TPU v7x, 32 devices: a whole 2x2x4 slice. The times are simulated.
32 devices in a mesh: gx: 4 (over x, core), gy: 8 (over z, y).
Axes of the slice: x: 2, y: 2, z: 4, core: 2. Of those that a mesh axis runs over, the one named last changes fastest.
Arguments:
- tokens: bfloat16 [16384, 1280], P(('gx', 'gy')), may hold values from -6 to 6
- out_grad: bfloat16 [16384, 1280], P(('gx', 'gy')), may hold values from -400 to 400
- segments: int32 [32, 512], P(('gx', 'gy')), may hold values from 0 to 7, never falling along the last dimension, each value on 1 to 256 neighbouring positions
- pos_rows: int32 [16384], P(('gx', 'gy')), may hold values from 0 to 15
- pos_cols: int32 [16384], P(('gx', 'gy')), may hold values from 0 to 15
- row_table: bfloat16 [16, 1280], replicated, may hold values from -4 to 4
- col_table: bfloat16 [16, 1280], replicated, may hold values from -4 to 4
- norm_gain: float32 [1280], replicated, may hold values from 0.25 to 1.75
- master_up: float32 [1280, 2560], P('gx'), may hold values from -0.15625 to 0.15625
- master_down: float32 [1280, 2560], P('gx'), may hold values from -0.125 to 0.125
- moment_up: float32 [1280, 2560], P('gx'), may hold values from -6 to 6
- moment_down: float32 [1280, 2560], P('gx'), may hold values from -6 to 6
Outputs:
- new_master_up: float32 [1280, 2560], P('gx')
- new_master_down: float32 [1280, 2560], P('gx')
- new_moment_up: float32 [1280, 2560], P('gx')
- new_moment_down: float32 [1280, 2560], P('gx')
Inputs may be any that keep to these rules, and one draw needn't show every extreme that they name: `segments`: each replica's 512 tokens hold all 8 images in order, each of 1 to 256 tokens.
All inputs are finite; a program needn't handle non-finite values.
Results may differ from a plain program's by a relative error of at most 0.02.
Values may be sent and summed in bfloat16 or wider, within the bound.
A program may use at most 128 MiB of HBM per device.

v0:
```python
import jax
import jax.numpy as jnp
from jax import lax
from jax.sharding import PartitionSpec as P

D = 1280
FF = 2560
GRID = 16
IMGS = 8


momentum_keep = 0.9
learn_rate = 0.01


def gelu_tanh(values):
    return (
        0.5
        * values
        * (1.0 + jnp.tanh(0.7978845608 * (values + 0.044715 * values * values * values)))
    )


def table_lookup(positions, table):
    onehot = (positions[:, None] == jnp.arange(GRID, dtype=jnp.int32)[None, :]).astype(jnp.bfloat16)
    return jnp.dot(onehot, table, preferred_element_type=jnp.float32)


def column_product(left, right):
    return lax.dot_general(
        left, right, (((0,), (0,)), ((), ())), preferred_element_type=jnp.float32
    )


def on_device(
    tokens,
    out_grad,
    segments,
    pos_rows,
    pos_cols,
    row_table,
    col_table,
    norm_gain,
    master_up,
    master_down,
    moment_up,
    moment_down,
):
    embedded = (
        tokens.astype(jnp.float32)
        + table_lookup(pos_rows, row_table)
        + table_lookup(pos_cols, col_table)
    )
    average = jnp.mean(embedded, axis=1, keepdims=True)
    centered = embedded - average
    variance = jnp.mean(centered * centered, axis=1, keepdims=True)
    normed = (centered * lax.rsqrt(variance + 1e-06) * norm_gain[None, :]).astype(jnp.bfloat16)
    member = (segments[0][:, None] == jnp.arange(IMGS, dtype=jnp.int32)[None, :]).astype(
        jnp.float32
    )
    per_image = 1.0 / jnp.sum(member, axis=0)
    token_weight = jnp.dot(member, per_image)
    weighted = (out_grad.astype(jnp.float32) * token_weight[:, None]).astype(jnp.bfloat16)
    left_cols = normed
    pre_act = jnp.dot(
        left_cols,
        lax.all_gather(master_up.astype(jnp.bfloat16), "gx", axis=0, tiled=True),
        preferred_element_type=jnp.float32,
    )
    hidden = gelu_tanh(pre_act).astype(jnp.bfloat16)
    left_cols = weighted
    hidden_grad = jnp.dot(
        left_cols,
        lax.all_gather(master_down.astype(jnp.bfloat16), "gx", axis=0, tiled=True),
        preferred_element_type=jnp.float32,
    )
    _, backward = jax.vjp(gelu_tanh, pre_act)
    pre_grad = backward(hidden_grad)[0].astype(jnp.bfloat16)
    group_sum = lax.psum_scatter(
        jnp.concatenate(
            [column_product(normed, pre_grad), column_product(weighted, hidden)], axis=1
        ).astype(jnp.bfloat16),
        "gx",
        scatter_dimension=0,
        tiled=True,
    )
    moments = jnp.concatenate([moment_up, moment_down], axis=1)
    masters = jnp.concatenate([master_up, master_down], axis=1)
    entries = 2.0 * D * FF
    grad_sum = lax.psum(group_sum, "gy").astype(jnp.float32)
    squares = lax.psum(jnp.sum(grad_sum * grad_sum), "gx")
    scale = lax.rsqrt(squares / entries + 1e-06)
    new_moments = momentum_keep * moments + scale * grad_sum
    new_masters = masters - learn_rate * new_moments
    half = master_up.shape[1]
    return (
        new_masters[:, :half],
        new_masters[:, half:],
        new_moments[:, :half],
        new_moments[:, half:],
    )


def solution(mesh):
    in_specs = (
        P(("gx", "gy"), None),
        P(("gx", "gy"), None),
        P(("gx", "gy"), None),
        P(("gx", "gy")),
        P(("gx", "gy")),
        P(),
        P(),
        P(),
        P("gx", None),
        P("gx", None),
        P("gx", None),
        P("gx", None),
    )
    out_specs = (P("gx", None), P("gx", None), P("gx", None), P("gx", None))
    return jax.shard_map(
        on_device, mesh=mesh, in_specs=in_specs, out_specs=out_specs, check_vma=False
    )
```

profile of v0, /device:TPU:0, one launch (start us, length us, event | category | flops | bytes accessed | tf_op | source)
XLA Modules:
  0.0 415.3 jit_solution(13771108014682099399)
XLA Ops:
  7.2 0.0 copy-start
  7.2 0.0 copy-start.2
  7.2 0.0 all-gather.3.cloned.1.call-start
  7.2 3.4 convert_element_type.35
  10.6 0.0 copy-start.7
  10.7 0.0 copy-start.4
  10.7 0.0 copy-start.5
  10.7 0.0 all-gather.3.cloned.1.call-update
  10.7 0.0 copy-start.6
  10.7 0.0 all-gather.5.cloned.1.call-start
  10.7 0.0 copy-done.2
  10.8 1.3 convert_element_type.39
  12.1 0.0 all-gather.5.cloned.1.call-update
  12.1 0.0 reduce-scatter.2.cloned.1.call-start
  12.2 0.0 copy-done.7
  12.2 0.1 convert_reduce_fusion
  12.3 0.0 copy-done.4
  12.3 0.0 copy-done.5
  12.3 0.0 copy-start.9
  12.3 1.9 convolution_add_fusion.1
  14.2 0.0 copy-done
  14.2 0.0 copy-done.6
  14.2 0.7 fusion.32
  14.9 0.0 copy-start.3
  14.9 1.5 copy-done.3
  16.4 0.4 multiply_reduce_fusion
  16.8 0.1 fusion.16
  16.9 44.5 %all-gather.3.cloned.1.call-done = bf16[1280,2560]{1,0:T(8,128)(2,1)} async-done(((bf16[320,2560]{1,0:T(8,128)(2,1)}), bf16[1280,2560]{1,0:T(8,128)(2,1)}) %all-gather.3.cloned.1.call-update) | async-done | bytes 6553616 | tf_op jit(solution)/shard_map/all_gather | solution.py:67
  61.4 0.0 copy-done.9
  61.4 0.0 copy-start.8
  61.4 6.7 %fusion.28 = f32[512,2560]{1,0:T(8,128)S(1)} fusion(bf16[1280,2560]{1,0:T(8,128)(2,1)} %all-gather.3.cloned.1.call-done, f32[512,1280]{1,0:T(8,128)} %copy-done.3, f32[1280]{0:T(1024)S(1)} %copy-done.9, f32[512]{0:T(512)S(1)} %add_rsqrt_fusion, f32[512]{0:T(512)S(1)} %broadcast_multiply_fusion), kind=kOutput, calls=%fused_computation.51 | convolution fusion | flops 3358064640 | bytes 14427136 | tf_op jit(solution)/shard_map/dot_general | solution.py:65
  68.1 0.0 copy-start.10
  68.1 2.4 copy-done.10
  70.5 0.0 copy-done.8
  70.5 6.0 %convolution_convert_fusion = bf16[1280,2560]{1,0:T(8,128)(2,1)} fusion(f32[512,2560]{1,0:T(8,128)S(1)} %fusion.28, bf16[512,1280]{1,0:T(8,128)(2,1)S(1)} %copy-done.8, f32[512]{0:T(512)S(1)} %bitcast.11), kind=kOutput, calls=%fused_computation.1 | convolution fusion | flops 3372482560 | bytes 13109248 | tf_op jit(solution)/shard_map/dot_general | solution.py:30
  76.4 35.0 %all-gather.5.cloned.1.call-done = bf16[1280,2560]{1,0:T(8,128)(2,1)} async-done(((bf16[320,2560]{1,0:T(8,128)(2,1)}), bf16[1280,2560]{1,0:T(8,128)(2,1)}) %all-gather.5.cloned.1.call-update) | async-done | bytes 6553616 | tf_op jit(solution)/shard_map/all_gather | solution.py:74
  111.4 14.9 %convolution_convert_fusion.1 = bf16[1280,2560]{1,0:T(8,128)(2,1)} fusion(f32[512,2560]{1,0:T(8,128)} %copy-done.10, bf16[1280,2560]{1,0:T(8,128)(2,1)} %all-gather.5.cloned.1.call-done, bf16[512,1280]{1,0:T(8,128)(2,1)} %param.13, f32[512]{0:T(512)S(1)} %bitcast.12, f32[512,1280]{1,0:T(8,128)} %copy-done.3, f32[1280]{0:T(1024)S(1)} %copy-done.9, ...), kind=kOutput, calls=%fused_computation.2 | convolution fusion | flops 6750208000 | bytes 22293504 | tf_op jit(solution)/shard_map/dot_general | solution.py:30
  126.3 12.2 %pad_maximum_fusion = bf16[1280,5120]{1,0:T(8,128)(2,1)} fusion(bf16[1280,2560]{1,0:T(8,128)(2,1)} %convolution_convert_fusion, bf16[1280,2560]{1,0:T(8,128)(2,1)} %convolution_convert_fusion.1), kind=kLoop, calls=%fused_computation | loop fusion | flops 26214400 | bytes 26214400 | tf_op jit(solution)/shard_map/concatenate | solution.py:80
  138.6 0.0 reduce-scatter.2.cloned.1.call-update
  138.6 0.2 all-reduce.2.cloned.1.call-start
  138.8 102.4 %reduce-scatter.2.cloned.1.call-done = bf16[320,5120]{1,0:T(8,128)(2,1)} async-done(((bf16[1280,5120]{1,0:T(8,128)(2,1)}), bf16[320,5120]{1,0:T(8,128)(2,1)}) %reduce-scatter.2.cloned.1.call-update) | async-done | bytes 3276816 | tf_op jit(solution)/shard_map/reduce_scatter | solution.py:79
  241.2 0.0 all-reduce.2.cloned.1.call-update
  241.3 136.6 %all-reduce.2.cloned.1.call-done = bf16[320,5120]{1,0:T(8,128)(2,1)} async-done(((bf16[320,5120]{1,0:T(8,128)(2,1)}), bf16[320,5120]{1,0:T(8,128)(2,1)}) %all-reduce.2.cloned.1.call-update) | async-done | bytes 3276816 | tf_op jit(solution)/shard_map/psum | solution.py:90
  377.9 4.2 %fusion = f32[]{:T(128)} fusion(bf16[320,5120]{1,0:T(8,128)(2,1)} %all-reduce.2.cloned.1.call-done), kind=kLoop, calls=%fused_computation.9 | loop fusion | flops 4915199 | bytes 3276804 | tf_op jit(solution)/shard_map/reduce_sum | solution.py:91
  382.1 7.4 %psum.15 = f32[]{:T(128)} all-reduce(f32[]{:T(128)} %fusion), channel_id=1, replica_groups=mesh['gx'=4,'gy'=8] {'gx'}, use_global_device_ids=true, to_apply=%region_6.0 | all-reduce | flops 1 | bytes 8 | tf_op jit(solution)/shard_map/psum | solution.py:91
  390.2 8.7 %maximum_subtract_fusion = (f32[320,5120]{1,0:T(8,128)}, f32[320,5120]{1,0:T(8,128)}) fusion(f32[320,2560]{1,0:T(8,128)S(1)} %copy-done.2, f32[320,2560]{1,0:T(8,128)} %param.20, bf16[320,5120]{1,0:T(8,128)(2,1)} %all-reduce.2.cloned.1.call-done, f32[]{:T(128)S(6)} %rsqrt.12, f32[320,2560]{1,0:T(8,128)} %param.23, f32[320,2560]{1,0:T(8,128)} %param.22), kind=kLoop, calls=%fused_computation.11 | loop fusion | flops 13107200 | bytes 29491204 | tf_op jit(solution)/shard_map/sub | solution.py:94
  398.9 9.9 %fusion.30 = (f32[320,2560]{1,0:T(8,128)}, f32[320,2560]{1,0:T(8,128)}, f32[320,2560]{1,0:T(8,128)}, f32[320,2560]{1,0:T(8,128)}) fusion(f32[320,5120]{1,0:T(8,128)} %get-tuple-element.5, f32[320,5120]{1,0:T(8,128)} %get-tuple-element.4), kind=kLoop, calls=%fused_computation.52 | loop fusion | bytes 26214400 | tf_op jit(solution)/shard_map/slice | solution.py:100
  408.8 0.0 copy-done.1
  (3 shorter events, 0.0 us)
Async XLA Ops:
  7.2 7.0 %copy-start = (bf16[16,1280]{1,0:T(8,128)(2,1)S(1)}, bf16[16,1280]{1,0:T(8,128)(2,1)}, u32[]{:S(2)}) copy-start(bf16[16,1280]{1,0:T(8,128)(2,1)} %param.18) | copy-start | bytes 122884
  7.2 3.6 copy-start.2
  7.2 54.2 %all-gather.3.cloned.1.call-start = ((), (), s32[]{:S(2)}) async-start(), calls=%async_computation.1 | async-start | bytes 8192000 | tf_op jit(solution)/shard_map/all_gather | solution.py:67
  10.6 1.5 copy-start.7
  10.7 1.6 copy-start.4
  10.7 1.6 copy-start.5
  10.7 3.5 copy-start.6
  10.7 100.7 %all-gather.5.cloned.1.call-start = ((), (), s32[]{:S(2)}) async-start(), calls=%async_computation.2 | async-start | bytes 8192000 | tf_op jit(solution)/shard_map/all_gather | solution.py:74
  12.1 229.1 %reduce-scatter.2.cloned.1.call-start = ((), (), s32[]{:S(2)}) async-start(), calls=%async_computation.3 | async-start | bytes 16384000 | tf_op jit(solution)/shard_map/reduce_scatter | solution.py:79
  12.3 49.1 %copy-start.9 = (f32[1280]{0:T(1024)S(1)}, f32[1280]{0:T(1024)}, u32[]{:S(2)}) copy-start(f32[1280]{0:T(1024)} %param.19) | copy-start | bytes 15364
  14.9 1.5 copy-start.3
  61.4 9.1 %copy-start.8 = (bf16[512,1280]{1,0:T(8,128)(2,1)S(1)}, bf16[512,1280]{1,0:T(8,128)(2,1)}, u32[]{:S(2)}) copy-start(bf16[512,1280]{1,0:T(8,128)(2,1)} %param.13) | copy-start | bytes 3932164
  68.1 2.4 copy-start.10
  138.6 239.3 %all-reduce.2.cloned.1.call-start = ((), (), s32[]{:S(2)}) async-start(), calls=%async_computation.4 | async-start | bytes 6553600 | tf_op jit(solution)/shard_map/psum | solution.py:90
  398.9 9.9 %copy-start.1 = (bf16[16,1280]{1,0:T(8,128)(2,1)S(1)}, bf16[16,1280]{1,0:T(8,128)(2,1)}, u32[]{:S(2)}) copy-start(bf16[16,1280]{1,0:T(8,128)(2,1)} %param.18) | copy-start | bytes 122884
Sparse Core Ops, SparseCore 0:
  10.8 50.5 all-gather.2
  63.5 47.8 all-gather.4
  138.7 102.5 reduce-scatter.1
  244.8 133.0 all-reduce.1
where the time goes:
time: 416 us; the launch traced here: 415 us
  waiting for transfers between devices  319 us (77%)
  other arithmetic  30.4 us (7%)
  matrix products  30.2 us (7%)
  between operations  14.6 us (4%)
  local copies, waits for them, and re-layouts  13.8 us (3%)
  blocking collectives  7.43 us (2%)
    psum x1, waiting for transfers between devices, on_device(): grad_sum = lax.psum(group_sum, 'gy').astype(jnp.float32)  137 us
    reduce_scatter x1, waiting for transfers between devices, on_device(): lax.psum_scatter(jnp.concatenate([column_product(normed, pre_grad), colum...  102 us
    all_gather x1, waiting for transfers between devices, on_device(): lax.all_gather(master_up.astype(jnp.bfloat16), 'gx', axis=0, tiled=True)  44.5 us
    all_gather x1, waiting for transfers between devices, on_device(): lax.all_gather(master_down.astype(jnp.bfloat16), 'gx', axis=0, tiled=True)  35 us
    dot_general x2, matrix products, column_product(): lax.dot_general(left, right, (((0,), (0,)), ((), ())), preferred_element_...  20.8 us
    concatenate x1, other arithmetic, on_device(): jnp.concatenate([column_product(normed, pre_grad), column_product(weighte...  12.2 us
    slice x1, local copies, waits for them, and re-layouts, on_device(): new_moments[:, half:]  9.88 us
    sub x1, other arithmetic, on_device(): new_masters = masters - learn_rate * new_moments  8.66 us
  transfers between devices with their start and end apart: 4, of which 4 were waited for; matrix products, arithmetic and copies ran while one was open for 4% of the time, Pallas kernels for 0%

commit v1 on v0

v1 whole, which is shorter than its diff:
```python
import functools

import jax
import jax.numpy as jnp
from jax import lax
from jax.experimental import pallas as pl
from jax.experimental.pallas import tpu as pltpu
from jax.sharding import PartitionSpec as P

momentum_keep = 0.9
learn_rate = 0.01
MESH = pl.DeviceIdType.MESH
VMEM = pltpu.VMEM
VMEM_LIMIT = 60 * 1024 * 1024
CORES = 2
PAIR = 2
PARTS = 2
Q = 2
S = 4


def gelu_tanh(values):
    return (
        0.5
        * values
        * (1.0 + jnp.tanh(0.7978845608 * (values + 0.044715 * values * values * values)))
    )


class Copies:
    def __init__(self, send, recv):
        self.send, self.recv, self.count, self.all = send, recv, 0, []

    def start(self, src, dst, device):
        copy = pltpu.make_async_remote_copy(
            src_ref=src,
            dst_ref=dst,
            send_sem=self.send.at[self.count],
            recv_sem=self.recv.at[self.count],
            device_id=device,
            device_id_type=MESH,
        )
        copy.start()
        self.count += 1
        self.all.append(copy)
        return copy

    def finish(self):
        for copy in self.all:
            copy.wait_send()


def greet(devices):
    barrier = pltpu.get_barrier_semaphore()
    for device in devices:
        pl.semaphore_signal(barrier, inc=1, device_id=device, device_id_type=MESH)
    pl.semaphore_wait(barrier, len(devices))


def place():
    gx, gy = lax.axis_index("gx"), lax.axis_index("gy")
    return gx, gy, gx // CORES, lax.rem(gx, CORES), gy // PAIR, lax.rem(gy, PAIR)


def gather_kernel(
    shard, tokens, out_grad, seg, rows, cols, table, gain, full, normed, weighted, send, recv
):
    gx, gy, x, c, h, l = place()
    partner = (x * CORES + 1 - c, gy)
    across = ((1 - x) * CORES + c, gy)
    diagonal = ((1 - x) * CORES + 1 - c, gy)
    beside = (gx, h * PAIR + 1 - l)
    greet([partner, across, diagonal, beside])
    copies = Copies(send, recv)
    depth = shard.shape[2]
    step = depth // S
    straight, crossed = [], []
    for s in range(S):
        part = pl.ds(s * step, step)
        straight.append(
            copies.start(shard.at[c, l, part], full.at[l, gx, part], across)
        )
        crossed.append(
            copies.start(shard.at[1 - c, l, part], full.at[l, gx, part], diagonal)
        )
    near = [copies.start(shard.at[1 - c, u], full.at[u, gx], partner) for u in range(PARTS)]
    for u in range(PARTS):
        full[u, gx] = shard[c, u]

    count = tokens.shape[0]
    grid = table.shape[0] // 2
    lanes = lax.broadcasted_iota(jnp.int32, (count, 128), 1)
    sizes = jnp.sum((seg[...] == lanes).astype(jnp.float32), axis=0, keepdims=True)
    per_image = 1.0 / jnp.maximum(sizes, 1.0)
    tile = 64

    @pl.loop(0, count // tile)
    def _(i):
        own = pl.ds(pl.multiple_of(i * tile, tile), tile)
        hot = lax.broadcasted_iota(jnp.int32, (tile, 2 * grid), 1)
        hot = ((hot == rows[own, :]) | (hot == cols[own, :] + grid)).astype(jnp.float32)
        embedded = tokens[own, :].astype(jnp.float32) + jnp.dot(
            hot.astype(jnp.bfloat16), table[...], preferred_element_type=jnp.float32
        )
        average = jnp.mean(embedded, axis=1, keepdims=True)
        centered = embedded - average
        variance = jnp.mean(centered * centered, axis=1, keepdims=True)
        normed[c, own, :] = (centered * lax.rsqrt(variance + 1e-06) * gain[...]).astype(
            jnp.bfloat16
        )
        lane = lax.broadcasted_iota(jnp.int32, (tile, 128), 1)
        member = (seg[own, :] == lane).astype(jnp.float32)
        weight = jnp.sum(member * per_image, axis=1, keepdims=True)
        weighted[c, own, :] = (out_grad[own, :].astype(jnp.float32) * weight).astype(jnp.bfloat16)

    shared = [
        copies.start(normed.at[c], normed.at[c], partner),
        copies.start(weighted.at[c], weighted.at[c], partner),
    ]
    passed = []
    for s in range(S):
        part = pl.ds(s * step, step)
        for arrived, owner in ((straight[s], across[0]), (crossed[s], diagonal[0])):
            arrived.wait_recv()
            piece = full.at[l, owner, part]
            passed.append(copies.start(piece, piece, beside))
    for copy in near + shared + passed:
        copy.wait_recv()
    copies.finish()


def reduce_kernel(
    norm_t, weight_t, pre_grad, hidden, out, squares,
    s1, r1, keep, s2, r2, s3, r3, whole, ss, ss_s, ss_r, send, recv,
):
    gx, gy, x, c, h, l = place()
    levels = lax.axis_size("gy") // PAIR
    partner = (x * CORES + 1 - c, gy)
    across = ((1 - x) * CORES + c, gy)
    beside = (gx, h * PAIR + 1 - l)
    ahead = [lax.rem(h + k, levels) for k in range(levels)]
    behind = [lax.rem(h + levels - k, levels) for k in range(levels)]
    above = [(gx, ahead[k] * PAIR + l) for k in range(levels)]
    greet([partner, across, beside] + above[1:])
    copies = Copies(send, recv)
    lefts, rights = (norm_t, weight_t), (pre_grad, hidden)
    block, width = s1.shape[3], s1.shape[4]
    deep = block // levels

    def product(p, q, at_x, at_l):
        own = pl.ds(pl.multiple_of((at_x * PAIR + at_l) * block, 16), block)
        return jnp.dot(
            lefts[p][own, :],
            rights[p][:, q * width : (q + 1) * width],
            preferred_element_type=jnp.float32,
        )

    first = {}
    targets = (across, beside)
    for q in range(Q):
        for slot in range(2):
            for p in range(PARTS):
                at = (1 - x, 1 - l) if slot == 0 else ((1 - x, l), (x, 1 - l))[p]
                s1[q, p, slot] = product(p, q, *at).astype(jnp.bfloat16)
                first[q, p, slot] = copies.start(
                    s1.at[q, p, slot], r1.at[q, p, slot], targets[p]
                )
    for q in range(Q):
        for slot in range(2):
            for p in range(PARTS):
                at = (x, l) if slot == 1 else ((x, 1 - l), (1 - x, l))[p]
                keep[q, p, slot] = product(p, q, *at)

    second = {}
    for q in range(Q):
        for p in range(PARTS):
            first[q, p, 0].wait_recv()
            s2[q, p] = (keep[q, p, 0] + r1[q, p, 0].astype(jnp.float32)).astype(jnp.bfloat16)
            second[q, p] = copies.start(s2.at[q, p], r2.at[q, p], targets[1 - p])

    third = {}
    for q in range(Q):
        for p in range(PARTS):
            first[q, p, 1].wait_recv()
            second[q, p].wait_recv()
            total = (
                keep[q, p, 1] + r1[q, p, 1].astype(jnp.float32) + r2[q, p].astype(jnp.float32)
            )
            keep[q, p, 1] = total
            for level in range(levels):
                s3[q, level, p] = total[level * deep : (level + 1) * deep].astype(jnp.bfloat16)
        for k in range(1, levels):
            third[q, k] = copies.start(s3.at[q, ahead[k]], r3.at[q, h], above[k])

    spread, passed = {}, []
    ss[...] = jnp.zeros_like(ss)
    mine = pl.ds(pl.multiple_of(h * deep, 16), deep)
    for q in range(Q):
        for k in range(1, levels):
            third[q, k].wait_recv()
        for p in range(PARTS):
            total = keep[q, p, 1, mine, :]
            for k in range(1, levels):
                total = total + r3[q, behind[k], p].astype(jnp.float32)
            whole[l, q, h, p] = total.astype(jnp.bfloat16)
            power = jnp.sum((total * total).reshape(deep // 8, 8, width), axis=0)
            for lane in range(width // 128):
                ss[...] += power[:, lane * 128 : (lane + 1) * 128]
        piece = whole.at[l, q, h]
        for k in range(1, levels):
            spread[q, k] = copies.start(piece, piece, above[k])
        passed.append(copies.start(piece, piece, beside))

    ss_s[0] = ss[...]
    waits = [copies.start(ss_s.at[0], ss_r.at[h], above[k]) for k in range(1, levels)]
    ss_r[h] = ss[...]
    for copy in waits:
        copy.wait_recv()
    running = ss_r[0]
    for level in range(1, levels):
        running = running + ss_r[level]
    for turn, target in enumerate((beside, across, partner)):
        ss_s[1 + turn] = running
        copies.start(ss_s.at[1 + turn], ss_r.at[levels + turn], target).wait_recv()
        running = running + ss_r[levels + turn]
    squares[...] = running

    for q in range(Q):
        for k in range(1, levels):
            spread[q, k].wait_recv()
            piece = whole.at[l, q, behind[k]]
            passed.append(copies.start(piece, piece, beside))
    for copy in passed:
        copy.wait_recv()
    last = [copies.start(whole.at[1 - c, q], out.at[c, q], partner) for q in range(Q)]
    for q in range(Q):
        out[c, q] = whole[c, q]
    for copy in last:
        copy.wait_recv()
    copies.finish()


def update_kernel(
    entries, grads, squares, up, down, moment_up, moment_down, new_up, new_down, new_mu, new_md
):
    scale = lax.rsqrt(jnp.sum(squares[...]) / entries + 1e-06)
    width = grads.shape[5]
    for q in range(Q):
        at = slice(q * width, (q + 1) * width)
        for p, old, moment, new, new_moment in (
            (0, up, moment_up, new_up, new_mu),
            (1, down, moment_down, new_down, new_md),
        ):
            fresh = momentum_keep * moment[:, at] + scale * grads[0, q, 0, p].astype(jnp.float32)
            new_moment[:, at] = fresh
            new[:, at] = old[:, at] - learn_rate * fresh


def cost(flops, moved):
    return pl.CostEstimate(flops=flops, bytes_accessed=moved, transcendentals=0)


def kernel_plan(
    tokens, out_grad, segments, pos_rows, pos_cols, row_table, col_table, norm_gain,
    master_up, master_down, moment_up, moment_down,
):
    bf16, f32 = jnp.bfloat16, jnp.float32
    shape = jax.ShapeDtypeStruct
    count, width = tokens.shape
    depth, hidden_units = master_up.shape
    gx, gy = lax.axis_size("gx"), lax.axis_size("gy")
    levels = gy // PAIR
    half = hidden_units // CORES
    shard = jnp.stack(
        [
            jnp.stack([m[:, i * half : (i + 1) * half].astype(bf16) for m in (master_up, master_down)])
            for i in range(CORES)
        ]
    )
    vm = pl.BlockSpec(memory_space=VMEM)
    n_copies = 4 * S + 4
    full, normed, weighted = pl.pallas_call(
        gather_kernel,
        out_shape=(
            shape((PARTS, gx, depth, half), bf16),
            shape((CORES, count, width), bf16),
            shape((CORES, count, width), bf16),
        ),
        in_specs=[vm] * 8,
        out_specs=(vm, vm, vm),
        scratch_shapes=[
            pltpu.SemaphoreType.DMA((n_copies,)),
            pltpu.SemaphoreType.DMA((n_copies,)),
        ],
        cost_estimate=cost(0, 4 * shard.size),
        compiler_params=pltpu.CompilerParams(
            collective_id=0, has_side_effects=True, vmem_limit_bytes=VMEM_LIMIT
        ),
    )(
        shard,
        tokens,
        out_grad,
        segments.reshape(count, 1),
        pos_rows.reshape(count, 1),
        pos_cols.reshape(count, 1),
        jnp.concatenate([row_table, col_table], axis=0),
        norm_gain.reshape(1, width),
    )
    both = CORES * count
    normed = normed.reshape(both, width)
    weighted = weighted.reshape(both, width)
    full = full.reshape(PARTS, width, half)
    pre_act = jnp.dot(normed, full[0], preferred_element_type=f32)
    hidden, backward = jax.vjp(gelu_tanh, pre_act)
    hidden_grad = jnp.dot(weighted, full[1], preferred_element_type=f32)
    pre_grad = backward(hidden_grad)[0].astype(bf16)
    hidden = hidden.astype(bf16)

    block = width // (gx // CORES) // PAIR
    cols = half // Q
    deep = block // levels
    n_copies = Q * (6 + 2 * (levels - 1) + levels + 1) + levels + 2
    grads, squares = pl.pallas_call(
        reduce_kernel,
        out_shape=(shape((CORES, Q, levels, PARTS, deep, cols), bf16), shape((8, 128), f32)),
        in_specs=[vm] * 4,
        out_specs=(vm, vm),
        scratch_shapes=[
            VMEM((Q, PARTS, 2, block, cols), bf16),
            VMEM((Q, PARTS, 2, block, cols), bf16),
            VMEM((Q, PARTS, 2, block, cols), f32),
            VMEM((Q, PARTS, block, cols), bf16),
            VMEM((Q, PARTS, block, cols), bf16),
            VMEM((Q, levels, PARTS, deep, cols), bf16),
            VMEM((Q, levels, PARTS, deep, cols), bf16),
            VMEM((PAIR, Q, levels, PARTS, deep, cols), bf16),
            VMEM((8, 128), f32),
            VMEM((4, 8, 128), f32),
            VMEM((levels + 3, 8, 128), f32),
            pltpu.SemaphoreType.DMA((n_copies,)),
            pltpu.SemaphoreType.DMA((n_copies,)),
        ],
        cost_estimate=cost(4 * both * width * half, 8 * both * width),
        compiler_params=pltpu.CompilerParams(
            collective_id=1, has_side_effects=True, vmem_limit_bytes=VMEM_LIMIT
        ),
    )(normed.T, weighted.T, pre_grad, hidden)

    flat = pl.BlockSpec((deep, half), lambda i, j: (i, j))
    return pl.pallas_call(
        functools.partial(update_kernel, 2.0 * width * hidden_units),
        grid=(levels, CORES),
        out_shape=(shape(master_up.shape, f32),) * 4,
        in_specs=[
            pl.BlockSpec((1, Q, 1, PARTS, deep, cols), lambda i, j: (j, 0, i, 0, 0, 0)),
            pl.BlockSpec((8, 128), lambda i, j: (0, 0)),
            flat, flat, flat, flat,
        ],
        out_specs=(flat,) * 4,
        cost_estimate=cost(8 * master_up.size, 34 * master_up.size),
        compiler_params=pltpu.CompilerParams(vmem_limit_bytes=VMEM_LIMIT),
    )(grads, squares, master_up, master_down, moment_up, moment_down)


def table_lookup(positions, table):
    onehot = (
        positions[:, None] == jnp.arange(table.shape[0], dtype=jnp.int32)[None, :]
    ).astype(jnp.bfloat16)
    return jnp.dot(onehot, table, preferred_element_type=jnp.float32)


def column_product(left, right):
    return lax.dot_general(
        left, right, (((0,), (0,)), ((), ())), preferred_element_type=jnp.float32
    )


def collective_plan(
    tokens, out_grad, segments, pos_rows, pos_cols, row_table, col_table, norm_gain,
    master_up, master_down, moment_up, moment_down,
):
    images = 8
    embedded = (
        tokens.astype(jnp.float32)
        + table_lookup(pos_rows, row_table)
        + table_lookup(pos_cols, col_table)
    )
    average = jnp.mean(embedded, axis=1, keepdims=True)
    centered = embedded - average
    variance = jnp.mean(centered * centered, axis=1, keepdims=True)
    normed = (centered * lax.rsqrt(variance + 1e-06) * norm_gain[None, :]).astype(jnp.bfloat16)
    member = (segments[0][:, None] == jnp.arange(images, dtype=jnp.int32)[None, :]).astype(
        jnp.float32
    )
    token_weight = jnp.dot(member, 1.0 / jnp.sum(member, axis=0))
    weighted = (out_grad.astype(jnp.float32) * token_weight[:, None]).astype(jnp.bfloat16)
    w_up = lax.all_gather(master_up.astype(jnp.bfloat16), "gx", axis=0, tiled=True)
    pre_act = jnp.dot(normed, w_up, preferred_element_type=jnp.float32)
    hidden, backward = jax.vjp(gelu_tanh, pre_act)
    w_down = lax.all_gather(master_down.astype(jnp.bfloat16), "gx", axis=0, tiled=True)
    hidden_grad = jnp.dot(weighted, w_down, preferred_element_type=jnp.float32)
    pre_grad = backward(hidden_grad)[0].astype(jnp.bfloat16)
    grads = [column_product(normed, pre_grad), column_product(weighted, hidden.astype(jnp.bfloat16))]
    group_sum = lax.psum_scatter(
        jnp.concatenate(grads, axis=1).astype(jnp.bfloat16), "gx", scatter_dimension=0, tiled=True
    )
    grad_sum = lax.psum(group_sum, "gy").astype(jnp.float32)
    squares = lax.psum(jnp.sum(grad_sum * grad_sum), "gx")
    entries = 2.0 * tokens.shape[1] * master_up.shape[1]
    scale = lax.rsqrt(squares / entries + 1e-06)
    half = master_up.shape[1]
    new_mu = momentum_keep * moment_up + scale * grad_sum[:, :half]
    new_md = momentum_keep * moment_down + scale * grad_sum[:, half:]
    return master_up - learn_rate * new_mu, master_down - learn_rate * new_md, new_mu, new_md


def solution(mesh):
    gx, gy = mesh.shape["gx"], mesh.shape["gy"]

    def on_device(*args):
        width, half = args[0].shape[1], args[8].shape[1] // CORES
        fits = (
            gx == 2 * CORES
            and gy % PAIR == 0
            and gy > PAIR
            and width % (gx * gy // CORES * 16) == 0
            and width % (gx * S * 16) == 0
            and half % (Q * 128) == 0
        )
        return (kernel_plan if fits else collective_plan)(*args)

    both, rows = P(("gx", "gy"), None), P("gx", None)
    return jax.shard_map(
        on_device,
        mesh=mesh,
        in_specs=(both, both, both, P(("gx", "gy")), P(("gx", "gy")), P(), P(), P())
        + (rows,) * 4,
        out_specs=(rows,) * 4,
        check_vma=False,
    )
```

time: 416 us -> 267 us (0.64)
  waiting for transfers between devices: 319 us -> 0 us
  Pallas kernels: 0 us -> 233 us
  other arithmetic: 30.4 us -> 5.33 us
  matrix products: 30.2 us -> 13 us
  between operations: 14.6 us -> 0.93 us
  blocking collectives: 7.43 us -> 0 us
    pallas_call x0 -> x3, Pallas kernels: none -> 233 us  [the longest x1 166 us: kernel_plan(): pl.pallas_call(reduce_kernel, out_shape=(shape((CORES, Q, levels, PARTS,...]
    psum x1 -> x0, waiting for transfers between devices: 137 us -> none  [on_device(): grad_sum = lax.psum(group_sum, 'gy').astype(jnp.float32)]
    reduce_scatter x1 -> x0, waiting for transfers between devices: 102 us -> none  [on_device(): lax.psum_scatter(jnp.concatenate([column_product(normed, pre_grad), colum...]
    all_gather x2 -> x0, waiting for transfers between devices: 79.5 us -> none  [the longest x1 44.5 us: on_device(): lax.all_gather(master_up.astype(jnp.bfloat16), 'gx', axis=0, tiled=True)]
    dot_general x6 -> x2, matrix products: 30.2 us -> 13 us  [the longest x1 9.4 us: kernel_plan(): pre_act = jnp.dot(normed, full[0], preferred_element_type=f32)]
    concatenate x1, other arithmetic: 12.2 us -> 0.64 us  [kernel_plan(): jnp.concatenate([row_table, col_table], axis=0)]
    reshape x0 -> x6, local copies, waits for them, and re-layouts: none -> 10.2 us  [the longest x1 4.38 us: kernel_plan(): normed = normed.reshape(both, width)]
    sub x1 -> x0, other arithmetic: 8.66 us -> none  [on_device(): new_masters = masters - learn_rate * new_moments]
  transfers between devices with their start and end apart: 4 -> 0, of which waited for: 4 -> 0; matrix products, arithmetic and copies ran while one was open for 4% -> 0% of each run, Pallas kernels for 0% -> 0%
where the time goes in v1:
time: 267 us; the launch traced here: 266 us
  Pallas kernels  233 us (87%)
  local copies, waits for them, and re-layouts  14.6 us (5%)
  matrix products  13 us (5%)
  other arithmetic  5.33 us (2%)
    pallas_call x1, Pallas kernels, kernel_plan(): pl.pallas_call(reduce_kernel, out_shape=(shape((CORES, Q, levels, PARTS,...  166 us
    pallas_call x1, Pallas kernels, kernel_plan(): pl.pallas_call(gather_kernel, out_shape=(shape((PARTS, gx, depth, half),...  54.1 us
    pallas_call x1, Pallas kernels, kernel_plan(): pl.pallas_call(functools.partial(update_kernel, 2.0 * width * hidden_unit...  12.5 us
    dot_general x1, matrix products, kernel_plan(): pre_act = jnp.dot(normed, full[0], preferred_element_type=f32)  9.4 us

profile of v1, /device:TPU:0, one launch (start us, length us, event | category | flops | bytes accessed | tf_op | source)
XLA Modules:
  0.0 266.3 jit_solution(2368483716950405028)
XLA Ops:
  0.6 0.0 copy-start
  0.6 2.2 convert.8
  2.9 0.1 slice_bitcast_fusion.3
  3.0 0.5 copy-done
  3.5 0.2 convert.9
  3.7 0.1 slice_bitcast_fusion.2
  3.8 0.3 maximum_bitcast_fusion
  4.1 0.0 copy-start.6
  4.1 0.0 copy-start.7
  4.1 0.0 copy-start.8
  4.2 0.0 copy-start.3
  4.2 0.0 copy-start.4
  4.2 0.0 copy-start.5
  4.2 2.0 pad_maximum_fusion.shard
  6.2 0.0 copy-done.6
  6.2 0.9 copy.18.seg
  7.0 0.0 copy-done.7
  7.1 0.9 copy.19.rows
  7.9 0.0 copy-done.8
  7.9 0.9 copy.20.cols
  8.8 0.0 copy-done.3
  8.8 0.0 copy-done.4
  8.8 0.6 pad_maximum_fusion.1.table
  9.4 0.0 copy-done.5
  9.4 0.6 reshape.34.gain
  10.0 54.1 %shard_map.147 = (bf16[2,4,320,1280]{3,2,1,0:T(8,128)(2,1)}, bf16[2,512,1280]{2,1,0:T(8,128)(2,1)}, bf16[2,512,1280]{2,1,0:T(8,128)(2,1)}) custom-call(bf16[2,2,320,1280]{3,2,1,0:T(8,128)(2,1)} %pad_maximum_fusion.shard, bf16[512,1280]{1,0:T(8,128)(2,1)} %tokens.1, bf16[512,1280]{1,0:T(8,128)(2,1)} %out_grad.1, s32[512,1]{1,0:T(8,128)} %copy.18.seg, ...), custom_call_target="tpu_custom_call" | custom-call | bytes 6553600 | tf_op jit(solution)/shard_map/pallas_call | solution.py:282
  64.2 0.0 copy-start.1
  64.2 3.5 %fusion.6 = (bf16[1,4,320,1280]{3,2,1,0:T(8,128)(2,1)S(1)}, bf16[1,4,320,1280]{3,2,1,0:T(8,128)(2,1)S(1)}) fusion(bf16[2,4,320,1280]{3,2,1,0:T(8,128)(2,1)} %get-tuple-element.11), kind=kLoop, calls=%fused_computation.19 | loop fusion | bytes 13107200 | tf_op jit(solution)/shard_map/slice | solution.py:315
  67.7 0.1 copy-done.1
  67.8 0.0 copy-start.2
  67.8 3.6 %fusion.7 = f32[1024,1280]{1,0:T(8,128)S(1)} fusion(bf16[1024,1280]{1,0:T(8,128)(2,1)S(1)} %bitcast.27, bf16[1280,1280]{1,0:T(8,128)(2,1)S(1)} %bitcast.26), kind=kOutput, calls=%fused_computation.20 | convolution fusion | flops 3355443200 | bytes 11141120 | tf_op jit(solution)/shard_map/dot_general | solution.py:315
  71.4 0.0 copy-done.2
  71.4 9.4 %multiply_convert_fusion = (bf16[1024,1280]{1,0:T(8,128)(2,1)}, bf16[1024,1280]{1,0:T(8,128)(2,1)}) fusion(f32[1024,1280]{1,0:T(8,128)S(1)} %fusion.7, bf16[1024,1280]{1,0:T(8,128)(2,1)S(1)} %bitcast.30, bf16[1280,1280]{1,0:T(8,128)(2,1)S(1)} %bitcast.25), kind=kOutput, calls=%fused_computation.10 | convolution fusion | flops 3389521920 | bytes 16384000 | tf_op jit(solution)/shard_map/dot_general | solution.py:313
  80.8 4.4 %copy.23 = bf16[1024,1280]{0,1:T(8,128)(2,1)} copy(bf16[1024,1280]{1,0:T(8,128)(2,1)} %bitcast.29) | data formatting | bytes 5242880 | tf_op jit(solution)/shard_map/reshape | solution.py:310
  85.2 2.6 copy.24
  87.8 165.8 %shard_map.148 = (bf16[2,2,4,2,80,640]{5,4,3,2,1,0:T(8,128)(2,1)}, f32[8,128]{1,0:T(8,128)}) custom-call(bf16[1280,1024]{1,0:T(8,128)(2,1)} %bitcast.31, bf16[1280,1024]{1,0:T(8,128)(2,1)} %bitcast.32, bf16[1024,1280]{1,0:T(8,128)(2,1)} %get-tuple-element.17.pre_grad, bf16[1024,1280]{1,0:T(8,128)(2,1)} %get-tuple-element.16.hidden), custom_call_target="tpu_custom_call" | custom-call | flops 6710886400 | bytes 10485760 | tf_op jit(solution)/shard_map/pallas_call | solution.py:323
  253.6 12.5 %shard_map.149 = (f32[320,2560]{1,0:T(8,128)}, f32[320,2560]{1,0:T(8,128)}, f32[320,2560]{1,0:T(8,128)}, f32[320,2560]{1,0:T(8,128)}) custom-call(bf16[2,2,4,2,80,640]{5,4,3,2,1,0:T(8,128)(2,1)} %get-tuple-element.12.grads, f32[8,128]{1,0:T(8,128)} %get-tuple-element.13.squares, f32[320,2560]{1,0:T(8,128)} %up.1, f32[320,2560]{1,0:T(8,128)} %down.1, ...), custom_call_target="tpu_custom_call" | custom-call | flops 6553600 | bytes 27852800 | tf_op jit(solution)/shard_map/pallas_call | solution.py:350
Async XLA Ops:
  0.6 2.9 %copy-start = (f32[320,2560]{1,0:T(8,128)S(1)}, f32[320,2560]{1,0:T(8,128)}, u32[]{:S(2)}) copy-start(f32[320,2560]{1,0:T(8,128)} %down.1) | copy-start | bytes 9830404
  4.1 2.1 copy-start.6
  4.1 2.9 %copy-start.7 = (s32[512]{0:T(512)S(1)}, s32[512]{0:T(512)}, u32[]{:S(2)}) copy-start(s32[512]{0:T(512)} %param.15) | copy-start | bytes 6148
  4.1 3.8 %copy-start.8 = (s32[512]{0:T(512)S(1)}, s32[512]{0:T(512)}, u32[]{:S(2)}) copy-start(s32[512]{0:T(512)} %param.16) | copy-start | bytes 6148
  4.2 4.6 %copy-start.3 = (bf16[16,1280]{1,0:T(8,128)(2,1)S(1)}, bf16[16,1280]{1,0:T(8,128)(2,1)}, u32[]{:S(2)}) copy-start(bf16[16,1280]{1,0:T(8,128)(2,1)} %param.18) | copy-start | bytes 122884
  4.2 4.6 %copy-start.4 = (bf16[16,1280]{1,0:T(8,128)(2,1)S(1)}, bf16[16,1280]{1,0:T(8,128)(2,1)}, u32[]{:S(2)}) copy-start(bf16[16,1280]{1,0:T(8,128)(2,1)} %param.17) | copy-start | bytes 122884
  4.2 5.2 %copy-start.5 = (f32[1280]{0:T(1024)S(1)}, f32[1280]{0:T(1024)}, u32[]{:S(2)}) copy-start(f32[1280]{0:T(1024)} %param.19) | copy-start | bytes 15364
  64.2 3.7 %copy-start.1 = (bf16[2,512,1280]{2,1,0:T(8,128)(2,1)S(1)}, bf16[2,512,1280]{2,1,0:T(8,128)(2,1)}, u32[]{:S(2)}) copy-start(bf16[2,512,1280]{2,1,0:T(8,128)(2,1)} %get-tuple-element.10) | copy-start | bytes 7864324
  67.8 3.6 %copy-start.2 = (bf16[2,512,1280]{2,1,0:T(8,128)(2,1)S(1)}, bf16[2,512,1280]{2,1,0:T(8,128)(2,1)}, u32[]{:S(2)}) copy-start(bf16[2,512,1280]{2,1,0:T(8,128)(2,1)} %get-tuple-element.9) | copy-start | bytes 7864324

commit v2 on v1

v2 whole, which is shorter than its diff:
```python
import functools

import jax
import jax.numpy as jnp
from jax import lax
from jax.experimental import pallas as pl
from jax.experimental.pallas import tpu as pltpu
from jax.sharding import PartitionSpec as P

momentum_keep = 0.9
learn_rate = 0.01
MESH = pl.DeviceIdType.MESH
VMEM = pltpu.VMEM
VMEM_LIMIT = 60 * 1024 * 1024
CORES = 2
PAIR = 2
PARTS = 2
Q = 5


def gelu_tanh(values):
    return (
        0.5
        * values
        * (1.0 + jnp.tanh(0.7978845608 * (values + 0.044715 * values * values * values)))
    )


class Copies:
    def __init__(self, send, recv):
        self.send, self.recv, self.count, self.all = send, recv, 0, []

    def start(self, src, dst, device):
        copy = pltpu.make_async_remote_copy(
            src_ref=src,
            dst_ref=dst,
            send_sem=self.send.at[self.count],
            recv_sem=self.recv.at[self.count],
            device_id=device,
            device_id_type=MESH,
        )
        copy.start()
        self.count += 1
        self.all.append(copy)
        return copy

    def finish(self):
        for copy in self.all:
            copy.wait_send()


def greet(devices):
    barrier = pltpu.get_barrier_semaphore()
    for device in devices:
        pl.semaphore_signal(barrier, inc=1, device_id=device, device_id_type=MESH)
    pl.semaphore_wait(barrier, len(devices))


def place():
    gx, gy = lax.axis_index("gx"), lax.axis_index("gy")
    return gx, gy, gx // CORES, lax.rem(gx, CORES), gy // PAIR, lax.rem(gy, PAIR)


def block_kernel(
    master_up, master_down, tokens, out_grad, seg, rows, cols, row_table, col_table, gain,
    out, squares,
    shard, full, normed, weighted, norm_t, weight_t, pre_grad, hidden,
    s1, r1, s2, r2, s3, r3, keep, whole, ss, ss_s, ss_r, send, recv,
):
    bf16, f32 = jnp.bfloat16, jnp.float32
    gx, gy, x, c, h, l = place()
    levels = lax.axis_size("gy") // PAIR
    partner = (x * CORES + 1 - c, gy)
    across = ((1 - x) * CORES + c, gy)
    diagonal = ((1 - x) * CORES + 1 - c, gy)
    beside = (gx, h * PAIR + 1 - l)
    odd = lax.rem(h, 2)
    neighbour = (gx, (h + 1 - 2 * odd) * PAIR + l)
    ahead = [lax.rem(h + k, levels) for k in range(levels)]
    behind = [lax.rem(h + levels - k, levels) for k in range(levels)]
    above = [(gx, ahead[k] * PAIR + l) for k in range(levels)]
    greet([partner, across, diagonal, beside] + above[1:])
    copies = Copies(send, recv)
    chunks, depth, width = shard.shape[1], shard.shape[3], shard.shape[4]
    count, features = tokens.shape
    block = s1.shape[3]
    deep = block // levels

    straight, crossed, near, passed = {}, {}, {}, {}

    def send_weights(q):
        for k in range(CORES):
            at = slice((k * chunks + q) * width, (k * chunks + q + 1) * width)
            shard[k, q, 0] = master_up[:, at].astype(bf16)
            shard[k, q, 1] = master_down[:, at].astype(bf16)
        mine = full.at[q, odd, gx]
        straight[q] = copies.start(shard.at[c, q, odd], mine, across)
        crossed[q] = copies.start(shard.at[1 - c, q, odd], mine, diagonal)
        near[q] = copies.start(shard.at[1 - c, q], full.at[q, :, gx], partner)
        for u in range(PARTS):
            full[q, u, gx] = shard[c, q, u]

    def pass_weights(q):
        for k, (arrived, owner) in enumerate(((straight[q], across[0]), (crossed[q], diagonal[0]))):
            arrived.wait_recv()
            piece = full.at[q, odd, owner]
            passed[q, k] = copies.start(piece, piece, neighbour)

    def column(row, lanes):
        return jnp.broadcast_to(row, (lanes, row.shape[1])).T

    def layer_norm():
        grid, tile = row_table.shape[0], 128
        images = lax.broadcasted_iota(jnp.int32, (128, count), 0)
        member = (jnp.broadcast_to(seg[...], (128, count)) == images).astype(f32)
        sizes = jnp.maximum(jnp.sum(member, axis=1, keepdims=True), 1.0)
        token_weight = jnp.sum(member * (1.0 / sizes), axis=0, keepdims=True)
        places = lax.broadcasted_iota(jnp.int32, (tile, 128), 1)
        for i in range(count // tile):
            at = slice(i * tile, (i + 1) * tile)
            own = pl.ds(pl.multiple_of(c * count + i * tile, tile), tile)
            embedded = tokens[at, :].astype(f32)
            for index, table in ((rows, row_table), (cols, col_table)):
                hot = column(index[:, at].astype(f32), 128)[:, :grid] == places[:, :grid].astype(f32)
                embedded += jnp.dot(
                    hot.astype(f32).astype(bf16), table[...], preferred_element_type=f32
                )
            average = jnp.mean(embedded, axis=1, keepdims=True)
            centered = embedded - average
            variance = jnp.mean(centered * centered, axis=1, keepdims=True)
            left = (centered * lax.rsqrt(variance + 1e-06) * gain[...]).astype(bf16)
            normed[own, :] = left
            norm_t[c, :, at] = left.T
            weight = column(token_weight[:, at], 128)[:, :1]
            right = (out_grad[at, :].astype(f32) * weight).astype(bf16)
            weighted[own, :] = right
            weight_t[c, :, at] = right.T

    def forward(q):
        near[q].wait_recv()
        for k in range(2):
            passed[q, k].wait_recv()
        up = full.at[q, 0]
        down = full.at[q, 1]
        tile = 256
        total = CORES * count

        @pl.loop(0, total // tile)
        def _(i):
            own = pl.ds(pl.multiple_of(i * tile, tile), tile)
            v = jnp.dot(
                normed[own, :], up[...].reshape(features, width), preferred_element_type=f32
            )
            grad = jnp.dot(
                weighted[own, :], down[...].reshape(features, width), preferred_element_type=f32
            )
            square = v * v
            t = jnp.tanh(0.7978845608 * (v + 0.044715 * (square * v)))
            rising = 0.5 * (1.0 + t)
            slope = 0.7978845608 * (1.0 + 3.0 * 0.044715 * square)
            hidden[q, own, :] = (v * rising).astype(bf16)
            pre_grad[q, own, :] = (grad * (rising + 0.5 * v * (1.0 - t * t) * slope)).astype(bf16)

    def product(p, q, at_x, at_l):
        own = pl.ds(pl.multiple_of((at_x * PAIR + at_l) * block, 16), block)
        left, right = ((norm_t, pre_grad), (weight_t, hidden))[p]
        return sum(
            jnp.dot(
                left[k, own, :],
                right[q, k * count : (k + 1) * count, :],
                preferred_element_type=f32,
            )
            for k in range(CORES)
        )

    first, second, third, spread, beyond, last = {}, {}, {}, {}, {}, {}
    targets = (across, beside)

    def send_first(q):
        for slot in range(2):
            for p in range(PARTS):
                at = (1 - x, 1 - l) if slot == 0 else ((1 - x, l), (x, 1 - l))[p]
                s1[q, p, slot] = product(p, q, *at).astype(bf16)
                first[q, p, slot] = copies.start(
                    s1.at[q, p, slot], r1.at[q, p, slot], targets[p]
                )

    def send_second(q):
        for p in range(PARTS):
            own = product(p, q, *((x, 1 - l), (1 - x, l))[p])
            first[q, p, 0].wait_recv()
            s2[q, p] = (own + r1[q, p, 0].astype(f32)).astype(bf16)
            second[q, p] = copies.start(s2.at[q, p], r2.at[q, p], targets[1 - p])

    def send_third(q):
        for p in range(PARTS):
            own = product(p, q, x, l)
            first[q, p, 1].wait_recv()
            second[q, p].wait_recv()
            total = own + r1[q, p, 1].astype(f32) + r2[q, p].astype(f32)
            for level in range(levels):
                piece = total[level * deep : (level + 1) * deep]
                keep[q, level, p] = piece
                s3[q, level, p] = piece.astype(bf16)
        for k in range(1, levels):
            third[q, k] = copies.start(s3.at[q, ahead[k]], r3.at[q, h], above[k])

    def send_whole(q):
        for k in range(1, levels):
            third[q, k].wait_recv()
        for p in range(PARTS):
            total = keep[q, h, p]
            for k in range(1, levels):
                total = total + r3[q, behind[k], p].astype(f32)
            whole[l, q, h, p] = total.astype(bf16)
            power = jnp.sum((total * total).reshape(deep // 8, 8, width), axis=0)
            for lane in range(width // 128):
                ss[...] += power[:, lane * 128 : (lane + 1) * 128]
        piece = whole.at[l, q, h]
        for k in range(1, levels):
            spread[q, k] = copies.start(piece, piece, above[k])
        beyond[q, 0] = copies.start(piece, piece, beside)

    def pass_whole(q):
        for k in range(1, levels):
            spread[q, k].wait_recv()
            piece = whole.at[l, q, behind[k]]
            beyond[q, k] = copies.start(piece, piece, beside)

    def send_last(q):
        for k in range(levels):
            beyond[q, k].wait_recv()
        last[q] = copies.start(whole.at[1 - c, q], out.at[c, q], partner)
        out[c, q] = whole[c, q]

    def add_squares():
        ss_s[0] = ss[...]
        waits = [copies.start(ss_s.at[0], ss_r.at[h], above[k]) for k in range(1, levels)]
        ss_r[h] = ss[...]
        for copy in waits:
            copy.wait_recv()
        running = ss_r[0]
        for level in range(1, levels):
            running = running + ss_r[level]
        for turn, target in enumerate((beside, across, partner)):
            ss_s[1 + turn] = running
            copies.start(ss_s.at[1 + turn], ss_r.at[levels + turn], target).wait_recv()
            running = running + ss_r[levels + turn]
        squares[...] = running

    ss[...] = jnp.zeros_like(ss)
    send_weights(0)
    send_weights(1)
    layer_norm()
    mine = pl.ds(pl.multiple_of(c * count, 128), count)
    shared = [
        copies.start(piece, piece, partner)
        for piece in (normed.at[mine], weighted.at[mine], norm_t.at[c], weight_t.at[c])
    ]
    pass_weights(0)
    for copy in shared:
        copy.wait_recv()
    for tick in range(chunks + 5):
        if tick + 2 < chunks:
            send_weights(tick + 2)
        if tick + 1 < chunks:
            pass_weights(tick + 1)
        steps = (forward, send_first), (send_second,), (send_third,), (send_whole,), (pass_whole,), (send_last,)
        for lag, actions in enumerate(steps):
            if 0 <= tick - lag < chunks:
                for action in actions:
                    action(tick - lag)
        if tick == chunks + 2:
            add_squares()
    for q in range(chunks):
        last[q].wait_recv()
    copies.finish()


def update_kernel(
    entries, grads, squares, up, down, moment_up, moment_down, new_up, new_down, new_mu, new_md
):
    scale = lax.rsqrt(jnp.sum(squares[...]) / entries + 1e-06)
    width = grads.shape[5]
    for q in range(Q):
        at = slice(q * width, (q + 1) * width)
        for p, old, moment, new, new_moment in (
            (0, up, moment_up, new_up, new_mu),
            (1, down, moment_down, new_down, new_md),
        ):
            fresh = momentum_keep * moment[:, at] + scale * grads[0, q, 0, p].astype(jnp.float32)
            new_moment[:, at] = fresh
            new[:, at] = old[:, at] - learn_rate * fresh


def cost(flops, moved):
    return pl.CostEstimate(flops=flops, bytes_accessed=moved, transcendentals=0)


def kernel_plan(
    tokens, out_grad, segments, pos_rows, pos_cols, row_table, col_table, norm_gain,
    master_up, master_down, moment_up, moment_down,
):
    bf16, f32 = jnp.bfloat16, jnp.float32
    shape = jax.ShapeDtypeStruct
    count, width = tokens.shape
    depth, hidden_units = master_up.shape
    gx, gy = lax.axis_size("gx"), lax.axis_size("gy")
    levels = gy // PAIR
    half = hidden_units // CORES
    both = CORES * count
    block = width // (gx // CORES) // PAIR
    cols = half // Q
    deep = block // levels
    vm = pl.BlockSpec(memory_space=VMEM)
    n_copies = Q * (11 + 2 * (levels - 1) + levels + 1) + 4 + levels + 2
    grads, squares = pl.pallas_call(
        block_kernel,
        out_shape=(shape((CORES, Q, levels, PARTS, deep, cols), bf16), shape((8, 128), f32)),
        in_specs=[vm] * 10,
        out_specs=(vm, vm),
        scratch_shapes=[
            VMEM((CORES, Q, PARTS, depth, cols), bf16),
            VMEM((Q, PARTS, gx, depth, cols), bf16),
            VMEM((both, width), bf16),
            VMEM((both, width), bf16),
            VMEM((CORES, width, count), bf16),
            VMEM((CORES, width, count), bf16),
            VMEM((Q, both, cols), bf16),
            VMEM((Q, both, cols), bf16),
            VMEM((Q, PARTS, 2, block, cols), bf16),
            VMEM((Q, PARTS, 2, block, cols), bf16),
            VMEM((Q, PARTS, block, cols), bf16),
            VMEM((Q, PARTS, block, cols), bf16),
            VMEM((Q, levels, PARTS, deep, cols), bf16),
            VMEM((Q, levels, PARTS, deep, cols), bf16),
            VMEM((Q, levels, PARTS, deep, cols), f32),
            VMEM((PAIR, Q, levels, PARTS, deep, cols), bf16),
            VMEM((8, 128), f32),
            VMEM((4, 8, 128), f32),
            VMEM((levels + 3, 8, 128), f32),
            pltpu.SemaphoreType.DMA((n_copies,)),
            pltpu.SemaphoreType.DMA((n_copies,)),
        ],
        cost_estimate=cost(8 * both * width * half, 8 * both * width),
        compiler_params=pltpu.CompilerParams(
            collective_id=0, has_side_effects=True, vmem_limit_bytes=VMEM_LIMIT
        ),
    )(
        master_up,
        master_down,
        tokens,
        out_grad,
        segments,
        pos_rows.reshape(1, count),
        pos_cols.reshape(1, count),
        row_table,
        col_table,
        norm_gain.reshape(1, width),
    )

    flat = pl.BlockSpec((deep, half), lambda i, j: (i, j))
    return pl.pallas_call(
        functools.partial(update_kernel, 2.0 * width * hidden_units),
        grid=(levels, CORES),
        out_shape=(shape(master_up.shape, f32),) * 4,
        in_specs=[
            pl.BlockSpec((1, Q, 1, PARTS, deep, cols), lambda i, j: (j, 0, i, 0, 0, 0)),
            pl.BlockSpec((8, 128), lambda i, j: (0, 0)),
            flat, flat, flat, flat,
        ],
        out_specs=(flat,) * 4,
        cost_estimate=cost(8 * master_up.size, 34 * master_up.size),
        compiler_params=pltpu.CompilerParams(vmem_limit_bytes=VMEM_LIMIT),
    )(grads, squares, master_up, master_down, moment_up, moment_down)


def table_lookup(positions, table):
    onehot = (
        positions[:, None] == jnp.arange(table.shape[0], dtype=jnp.int32)[None, :]
    ).astype(jnp.bfloat16)
    return jnp.dot(onehot, table, preferred_element_type=jnp.float32)


def column_product(left, right):
    return lax.dot_general(
        left, right, (((0,), (0,)), ((), ())), preferred_element_type=jnp.float32
    )


def collective_plan(
    tokens, out_grad, segments, pos_rows, pos_cols, row_table, col_table, norm_gain,
    master_up, master_down, moment_up, moment_down,
):
    images = 8
    embedded = (
        tokens.astype(jnp.float32)
        + table_lookup(pos_rows, row_table)
        + table_lookup(pos_cols, col_table)
    )
    average = jnp.mean(embedded, axis=1, keepdims=True)
    centered = embedded - average
    variance = jnp.mean(centered * centered, axis=1, keepdims=True)
    normed = (centered * lax.rsqrt(variance + 1e-06) * norm_gain[None, :]).astype(jnp.bfloat16)
    member = (segments[0][:, None] == jnp.arange(images, dtype=jnp.int32)[None, :]).astype(
        jnp.float32
    )
    token_weight = jnp.dot(member, 1.0 / jnp.sum(member, axis=0))
    weighted = (out_grad.astype(jnp.float32) * token_weight[:, None]).astype(jnp.bfloat16)
    w_up = lax.all_gather(master_up.astype(jnp.bfloat16), "gx", axis=0, tiled=True)
    pre_act = jnp.dot(normed, w_up, preferred_element_type=jnp.float32)
    hidden, backward = jax.vjp(gelu_tanh, pre_act)
    w_down = lax.all_gather(master_down.astype(jnp.bfloat16), "gx", axis=0, tiled=True)
    hidden_grad = jnp.dot(weighted, w_down, preferred_element_type=jnp.float32)
    pre_grad = backward(hidden_grad)[0].astype(jnp.bfloat16)
    grads = [column_product(normed, pre_grad), column_product(weighted, hidden.astype(jnp.bfloat16))]
    group_sum = lax.psum_scatter(
        jnp.concatenate(grads, axis=1).astype(jnp.bfloat16), "gx", scatter_dimension=0, tiled=True
    )
    grad_sum = lax.psum(group_sum, "gy").astype(jnp.float32)
    squares = lax.psum(jnp.sum(grad_sum * grad_sum), "gx")
    entries = 2.0 * tokens.shape[1] * master_up.shape[1]
    scale = lax.rsqrt(squares / entries + 1e-06)
    half = master_up.shape[1]
    new_mu = momentum_keep * moment_up + scale * grad_sum[:, :half]
    new_md = momentum_keep * moment_down + scale * grad_sum[:, half:]
    return master_up - learn_rate * new_mu, master_down - learn_rate * new_md, new_mu, new_md


def solution(mesh):
    gx, gy = mesh.shape["gx"], mesh.shape["gy"]

    def on_device(*args):
        width, half = args[0].shape[1], args[8].shape[1] // CORES
        fits = (
            gx == 2 * CORES
            and gy % PAIR == 0
            and gy > PAIR
            and args[0].shape[0] % 128 == 0
            and width % (gx * gy // CORES * 16) == 0
            and width % (gx * 16) == 0
            and gy // PAIR % 2 == 0
            and half % (Q * 128) == 0
        )
        return (kernel_plan if fits else collective_plan)(*args)

    both, rows = P(("gx", "gy"), None), P("gx", None)
    return jax.shard_map(
        on_device,
        mesh=mesh,
        in_specs=(both, both, both, P(("gx", "gy")), P(("gx", "gy")), P(), P(), P())
        + (rows,) * 4,
        out_specs=(rows,) * 4,
        check_vma=False,
    )
```

time: 267 us -> 173 us (0.65)
  Pallas kernels: 233 us -> 171 us
  local copies, waits for them, and re-layouts: 14.6 us -> 1.29 us
  matrix products: 13 us -> 0 us
  other arithmetic: 5.33 us -> 0 us
    pallas_call x2 -> x1, Pallas kernels: 220 us -> 158 us  [kernel_plan(): pl.pallas_call(block_kernel, out_shape=(shape((CORES, Q, levels, PARTS, d...]
    dot_general x2 -> x0, matrix products: 13 us -> none  [the longest x1 9.4 us: kernel_plan(): pre_act = jnp.dot(normed, full[0], preferred_element_type=f32)]
    reshape x5 -> x0, local copies, waits for them, and re-layouts: 9.57 us -> none  [the longest x1 4.38 us: kernel_plan(): normed = normed.reshape(both, width)]
    another operation x4 -> x0, other arithmetic: 4.69 us -> none
    slice x1 -> x0, local copies, waits for them, and re-layouts: 3.51 us -> none  [kernel_plan(): hidden_grad = jnp.dot(weighted, full[1], preferred_element_type=f32)]
where the time goes in v2:
time: 173 us
  Pallas kernels  171 us (99%)
    pallas_call x1, Pallas kernels, kernel_plan(): pl.pallas_call(block_kernel, out_shape=(shape((CORES, Q, levels, PARTS, d...  158 us
    pallas_call x1, Pallas kernels, kernel_plan(): pl.pallas_call(functools.partial(update_kernel, 2.0 * width * hidden_unit...  12.5 us

profile of v2, /device:TPU:0, one launch (start us, length us, event | category | flops | bytes accessed | tf_op | source)
XLA Modules:
  0.0 172.6 jit_solution(8169139489046149472)
XLA Ops:
  0.6 1.3 reshape.19.gain
  1.9 158.0 %shard_map.147 = (bf16[2,5,4,2,80,256]{5,4,3,2,1,0:T(8,128)(2,1)}, f32[8,128]{1,0:T(8,128)}) custom-call(f32[320,2560]{1,0:T(8,128)} %up.1, f32[320,2560]{1,0:T(8,128)} %down.1, bf16[512,1280]{1,0:T(8,128)(2,1)} %tokens.1, bf16[512,1280]{1,0:T(8,128)(2,1)} %out_grad.1, s32[1,512]{1,0:T(1,128)} %seg.1, s32[1,512]{1,0:T(1,128)} %bitcast.2, s32[1,512]{1,0:T(1,128)} %bitcast.3, ...), custom_call_target="tpu_custom_call" | custom-call | flops 13421772800 | bytes 10485760 | tf_op jit(solution)/shard_map/pallas_call | solution.py:317
  159.9 12.5 %shard_map.148 = (f32[320,2560]{1,0:T(8,128)}, f32[320,2560]{1,0:T(8,128)}, f32[320,2560]{1,0:T(8,128)}, f32[320,2560]{1,0:T(8,128)}) custom-call(bf16[2,5,4,2,80,256]{5,4,3,2,1,0:T(8,128)(2,1)} %get-tuple-element.6.grads, f32[8,128]{1,0:T(8,128)} %get-tuple-element.7.squares, f32[320,2560]{1,0:T(8,128)} %up.1, f32[320,2560]{1,0:T(8,128)} %down.1, ...), custom_call_target="tpu_custom_call" | custom-call | flops 6553600 | bytes 27852800 | tf_op jit(solution)/shard_map/pallas_call | solution.py:363

commit v3 on v2

--- a/solution.py
+++ b/solution.py
@@ -15,7 +15,6 @@
 CORES = 2
 PAIR = 2
 PARTS = 2
-Q = 5
 
 
 def gelu_tanh(values):
@@ -24,6 +23,12 @@
         * values
         * (1.0 + jnp.tanh(0.7978845608 * (values + 0.044715 * values * values * values)))
     )
+
+
+def chunk_widths(columns):
+    if columns % 256 or columns < 512:
+        return [128] * (columns // 128)
+    return [128] + [256] * (columns // 256 - 1) + [128]
 
 
 class Copies:
@@ -81,29 +86,34 @@
     above = [(gx, ahead[k] * PAIR + l) for k in range(levels)]
     greet([partner, across, diagonal, beside] + above[1:])
     copies = Copies(send, recv)
-    chunks, depth, width = shard.shape[1], shard.shape[3], shard.shape[4]
+    half = shard.shape[3]
+    widths = chunk_widths(half)
+    chunks = len(widths)
+    at = [pl.ds(sum(widths[:q]), widths[q]) for q in range(chunks)]
     count, features = tokens.shape
-    block = s1.shape[3]
+    block = s1.shape[2]
     deep = block // levels
 
     straight, crossed, near, passed = {}, {}, {}, {}
 
     def send_weights(q):
         for k in range(CORES):
-            at = slice((k * chunks + q) * width, (k * chunks + q + 1) * width)
-            shard[k, q, 0] = master_up[:, at].astype(bf16)
-            shard[k, q, 1] = master_down[:, at].astype(bf16)
-        mine = full.at[q, odd, gx]
-        straight[q] = copies.start(shard.at[c, q, odd], mine, across)
-        crossed[q] = copies.start(shard.at[1 - c, q, odd], mine, diagonal)
-        near[q] = copies.start(shard.at[1 - c, q], full.at[q, :, gx], partner)
+            start = k * half + at[q].start
+            shard[k, 0, :, at[q]] = master_up[:, start : start + widths[q]].astype(bf16)
+            shard[k, 1, :, at[q]] = master_down[:, start : start + widths[q]].astype(bf16)
+        mine = full.at[odd, gx, :, at[q]]
+        straight[q] = copies.start(shard.at[c, odd, :, at[q]], mine, across)
+        crossed[q] = copies.start(shard.at[1 - c, odd, :, at[q]], mine, diagonal)
+        near[q] = copies.start(
+            shard.at[1 - c, :, :, at[q]], full.at[:, gx, :, at[q]], partner
+        )
         for u in range(PARTS):
-            full[q, u, gx] = shard[c, q, u]
+            full[u, gx, :, at[q]] = shard[c, u, :, at[q]]
 
     def pass_weights(q):
         for k, (arrived, owner) in enumerate(((straight[q], across[0]), (crossed[q], diagonal[0]))):
             arrived.wait_recv()
-            piece = full.at[q, odd, owner]
+            piece = full.at[odd, owner, :, at[q]]
             passed[q, k] = copies.start(piece, piece, neighbour)
 
     def column(row, lanes):
@@ -117,11 +127,11 @@
         token_weight = jnp.sum(member * (1.0 / sizes), axis=0, keepdims=True)
         places = lax.broadcasted_iota(jnp.int32, (tile, 128), 1)
         for i in range(count // tile):
-            at = slice(i * tile, (i + 1) * tile)
+            span = slice(i * tile, (i + 1) * tile)
             own = pl.ds(pl.multiple_of(c * count + i * tile, tile), tile)
-            embedded = tokens[at, :].astype(f32)
+            embedded = tokens[span, :].astype(f32)
             for index, table in ((rows, row_table), (cols, col_table)):
-                hot = column(index[:, at].astype(f32), 128)[:, :grid] == places[:, :grid].astype(f32)
+                hot = column(index[:, span].astype(f32), 128)[:, :grid] == places[:, :grid].astype(f32)
                 embedded += jnp.dot(
                     hot.astype(f32).astype(bf16), table[...], preferred_element_type=f32
                 )
@@ -130,36 +140,35 @@
             variance = jnp.mean(centered * centered, axis=1, keepdims=True)
             left = (centered * lax.rsqrt(variance + 1e-06) * gain[...]).astype(bf16)
             normed[own, :] = left
-            norm_t[c, :, at] = left.T
-            weight = column(token_weight[:, at], 128)[:, :1]
-            right = (out_grad[at, :].astype(f32) * weight).astype(bf16)
+            norm_t[c, :, span] = left.T
+            weight = column(token_weight[:, span], 128)[:, :1]
+            right = (out_grad[span, :].astype(f32) * weight).astype(bf16)
             weighted[own, :] = right
-            weight_t[c, :, at] = right.T
+            weight_t[c, :, span] = right.T
 
     def forward(q):
         near[q].wait_recv()
         for k in range(2):
             passed[q, k].wait_recv()
-        up = full.at[q, 0]
-        down = full.at[q, 1]
         tile = 256
+        width = widths[q]
         total = CORES * count
 
         @pl.loop(0, total // tile)
         def _(i):
             own = pl.ds(pl.multiple_of(i * tile, tile), tile)
             v = jnp.dot(
-                normed[own, :], up[...].reshape(features, width), preferred_element_type=f32
+                normed[own, :], full[0, :, :, at[q]].reshape(features, width), preferred_element_type=f32
             )
             grad = jnp.dot(
-                weighted[own, :], down[...].reshape(features, width), preferred_element_type=f32
+                weighted[own, :], full[1, :, :, at[q]].reshape(features, width), preferred_element_type=f32
             )
             square = v * v
             t = jnp.tanh(0.7978845608 * (v + 0.044715 * (square * v)))
             rising = 0.5 * (1.0 + t)
             slope = 0.7978845608 * (1.0 + 3.0 * 0.044715 * square)
-            hidden[q, own, :] = (v * rising).astype(bf16)
-            pre_grad[q, own, :] = (grad * (rising + 0.5 * v * (1.0 - t * t) * slope)).astype(bf16)
+            hidden[own, at[q]] = (v * rising).astype(bf16)
+            pre_grad[own, at[q]] = (grad * (rising + 0.5 * v * (1.0 - t * t) * slope)).astype(bf16)
 
     def product(p, q, at_x, at_l):
         own = pl.ds(pl.multiple_of((at_x * PAIR + at_l) * block, 16), block)
@@ -167,7 +176,7 @@
         return sum(
             jnp.dot(
                 left[k, own, :],
-                right[q, k * count : (k + 1) * count, :],
+                right[k * count : (k + 1) * count, at[q]],
                 preferred_element_type=f32,
             )
             for k in range(CORES)
@@ -179,44 +188,46 @@
     def send_first(q):
         for slot in range(2):
             for p in range(PARTS):
-                at = (1 - x, 1 - l) if slot == 0 else ((1 - x, l), (x, 1 - l))[p]
-                s1[q, p, slot] = product(p, q, *at).astype(bf16)
+                where = (1 - x, 1 - l) if slot == 0 else ((1 - x, l), (x, 1 - l))[p]
+                s1[p, slot, :, at[q]] = product(p, q, *where).astype(bf16)
                 first[q, p, slot] = copies.start(
-                    s1.at[q, p, slot], r1.at[q, p, slot], targets[p]
+                    s1.at[p, slot, :, at[q]], r1.at[p, slot, :, at[q]], targets[p]
                 )
 
     def send_second(q):
         for p in range(PARTS):
             own = product(p, q, *((x, 1 - l), (1 - x, l))[p])
             first[q, p, 0].wait_recv()
-            s2[q, p] = (own + r1[q, p, 0].astype(f32)).astype(bf16)
-            second[q, p] = copies.start(s2.at[q, p], r2.at[q, p], targets[1 - p])
+            s2[p, :, at[q]] = (own + r1[p, 0, :, at[q]].astype(f32)).astype(bf16)
+            second[q, p] = copies.start(s2.at[p, :, at[q]], r2.at[p, :, at[q]], targets[1 - p])
 
     def send_third(q):
         for p in range(PARTS):
             own = product(p, q, x, l)
             first[q, p, 1].wait_recv()
             second[q, p].wait_recv()
-            total = own + r1[q, p, 1].astype(f32) + r2[q, p].astype(f32)
+            total = own + r1[p, 1, :, at[q]].astype(f32) + r2[p, :, at[q]].astype(f32)
             for level in range(levels):
                 piece = total[level * deep : (level + 1) * deep]
-                keep[q, level, p] = piece
-                s3[q, level, p] = piece.astype(bf16)
+                keep[level, p, :, at[q]] = piece
+                s3[level, p, :, at[q]] = piece.astype(bf16)
         for k in range(1, levels):
-            third[q, k] = copies.start(s3.at[q, ahead[k]], r3.at[q, h], above[k])
+            third[q, k] = copies.start(
+                s3.at[ahead[k], :, :, at[q]], r3.at[h, :, :, at[q]], above[k]
+            )
 
     def send_whole(q):
         for k in range(1, levels):
             third[q, k].wait_recv()
         for p in range(PARTS):
-            total = keep[q, h, p]
+            total = keep[h, p, :, at[q]]
             for k in range(1, levels):
-                total = total + r3[q, behind[k], p].astype(f32)
-            whole[l, q, h, p] = total.astype(bf16)
-            power = jnp.sum((total * total).reshape(deep // 8, 8, width), axis=0)
-            for lane in range(width // 128):
+                total = total + r3[behind[k], p, :, at[q]].astype(f32)
+            whole[l, h, p, :, at[q]] = total.astype(bf16)
+            power = jnp.sum((total * total).reshape(deep // 8, 8, widths[q]), axis=0)
+            for lane in range(widths[q] // 128):
                 ss[...] += power[:, lane * 128 : (lane + 1) * 128]
-        piece = whole.at[l, q, h]
+        piece = whole.at[l, h, :, :, at[q]]
         for k in range(1, levels):
             spread[q, k] = copies.start(piece, piece, above[k])
         beyond[q, 0] = copies.start(piece, piece, beside)
@@ -224,14 +235,16 @@
     def pass_whole(q):
         for k in range(1, levels):
             spread[q, k].wait_recv()
-            piece = whole.at[l, q, behind[k]]
+            piece = whole.at[l, behind[k], :, :, at[q]]
             beyond[q, k] = copies.start(piece, piece, beside)
 
     def send_last(q):
         for k in range(levels):
             beyond[q, k].wait_recv()
-        last[q] = copies.start(whole.at[1 - c, q], out.at[c, q], partner)
-        out[c, q] = whole[c, q]
+        last[q] = copies.start(
+            whole.at[1 - c, :, :, :, at[q]], out.at[c, :, :, :, at[q]], partner
+        )
+        out[c, :, :, :, at[q]] = whole[c, :, :, :, at[q]]
 
     def add_squares():
         ss_s[0] = ss[...]
@@ -250,7 +263,6 @@
 
     ss[...] = jnp.zeros_like(ss)
     send_weights(0)
-    send_weights(1)
     layer_norm()
     mine = pl.ds(pl.multiple_of(c * count, 128), count)
     shared = [
@@ -258,18 +270,21 @@
         for piece in (normed.at[mine], weighted.at[mine], norm_t.at[c], weight_t.at[c])
     ]
     pass_weights(0)
+    send_weights(1)
     for copy in shared:
         copy.wait_recv()
+    order = (
+        (0, forward), (5, send_last), (4, pass_whole), (3, send_whole),
+        (2, send_third), (1, send_second), (0, send_first),
+    )
     for tick in range(chunks + 5):
-        if tick + 2 < chunks:
-            send_weights(tick + 2)
-        if tick + 1 < chunks:
-            pass_weights(tick + 1)
-        steps = (forward, send_first), (send_second,), (send_third,), (send_whole,), (pass_whole,), (send_last,)
-        for lag, actions in enumerate(steps):
+        if 0 < tick and tick + 1 < chunks:
+            send_weights(tick + 1)
+        for lag, action in order:
             if 0 <= tick - lag < chunks:
-                for action in actions:
-                    action(tick - lag)
+                action(tick - lag)
+            if lag == 0 and action is forward and tick + 1 < chunks:
+                pass_weights(tick + 1)
         if tick == chunks + 2:
             add_squares()
     for q in range(chunks):
@@ -281,16 +296,13 @@
     entries, grads, squares, up, down, moment_up, moment_down, new_up, new_down, new_mu, new_md
 ):
     scale = lax.rsqrt(jnp.sum(squares[...]) / entries + 1e-06)
-    width = grads.shape[5]
-    for q in range(Q):
-        at = slice(q * width, (q + 1) * width)
-        for p, old, moment, new, new_moment in (
-            (0, up, moment_up, new_up, new_mu),
-            (1, down, moment_down, new_down, new_md),
-        ):
-            fresh = momentum_keep * moment[:, at] + scale * grads[0, q, 0, p].astype(jnp.float32)
-            new_moment[:, at] = fresh
-            new[:, at] = old[:, at] - learn_rate * fresh
+    for p, old, moment, new, new_moment in (
+        (0, up, moment_up, new_up, new_mu),
+        (1, down, moment_down, new_down, new_md),
+    ):
+        fresh = momentum_keep * moment[...] + scale * grads[0, 0, p].astype(jnp.float32)
+        new_moment[...] = fresh
+        new[...] = old[...] - learn_rate * fresh
 
 
 def cost(flops, moved):
@@ -310,32 +322,32 @@
     half = hidden_units // CORES
     both = CORES * count
     block = width // (gx // CORES) // PAIR
-    cols = half // Q
     deep = block // levels
+    chunks = len(chunk_widths(half))
     vm = pl.BlockSpec(memory_space=VMEM)
-    n_copies = Q * (11 + 2 * (levels - 1) + levels + 1) + 4 + levels + 2
+    n_copies = chunks * (11 + 2 * (levels - 1) + levels + 1) + 4 + levels + 2
     grads, squares = pl.pallas_call(
         block_kernel,
-        out_shape=(shape((CORES, Q, levels, PARTS, deep, cols), bf16), shape((8, 128), f32)),
+        out_shape=(shape((CORES, levels, PARTS, deep, half), bf16), shape((8, 128), f32)),
         in_specs=[vm] * 10,
         out_specs=(vm, vm),
         scratch_shapes=[
-            VMEM((CORES, Q, PARTS, depth, cols), bf16),
-            VMEM((Q, PARTS, gx, depth, cols), bf16),
+            VMEM((CORES, PARTS, depth, half), bf16),
+            VMEM((PARTS, gx, depth, half), bf16),
             VMEM((both, width), bf16),
             VMEM((both, width), bf16),
             VMEM((CORES, width, count), bf16),
             VMEM((CORES, width, count), bf16),
-            VMEM((Q, both, cols), bf16),
-            VMEM((Q, both, cols), bf16),
-            VMEM((Q, PARTS, 2, block, cols), bf16),
-            VMEM((Q, PARTS, 2, block, cols), bf16),
-            VMEM((Q, PARTS, block, cols), bf16),
-            VMEM((Q, PARTS, block, cols), bf16),
-            VMEM((Q, levels, PARTS, deep, cols), bf16),
-            VMEM((Q, levels, PARTS, deep, cols), bf16),
-            VMEM((Q, levels, PARTS, deep, cols), f32),
-            VMEM((PAIR, Q, levels, PARTS, deep, cols), bf16),
+            VMEM((both, half), bf16),
+            VMEM((both, half), bf16),
+            VMEM((PARTS, 2, block, half), bf16),
+            VMEM((PARTS, 2, block, half), bf16),
+            VMEM((PARTS, block, half), bf16),
+            VMEM((PARTS, block, half), bf16),
+            VMEM((levels, PARTS, deep, half), bf16),
+            VMEM((levels, PARTS, deep, half), bf16),
+            VMEM((levels, PARTS, deep, half), f32),
+            VMEM((PAIR, levels, PARTS, deep, half), bf16),
             VMEM((8, 128), f32),
             VMEM((4, 8, 128), f32),
             VMEM((levels + 3, 8, 128), f32),
@@ -365,7 +377,7 @@
         grid=(levels, CORES),
         out_shape=(shape(master_up.shape, f32),) * 4,
         in_specs=[
-            pl.BlockSpec((1, Q, 1, PARTS, deep, cols), lambda i, j: (j, 0, i, 0, 0, 0)),
+            pl.BlockSpec((1, 1, PARTS, deep, half), lambda i, j: (j, i, 0, 0, 0)),
             pl.BlockSpec((8, 128), lambda i, j: (0, 0)),
             flat, flat, flat, flat,
         ],
@@ -440,7 +452,7 @@
             and width % (gx * gy // CORES * 16) == 0
             and width % (gx * 16) == 0
             and gy // PAIR % 2 == 0
-            and half % (Q * 128) == 0
+            and half % 128 == 0
         )
         return (kernel_plan if fits else collective_plan)(*args)
 

time: 173 us -> 188 us (1.087)
  Pallas kernels: 171 us -> 184 us
    pallas_call x1, Pallas kernels: 158 us -> 172 us  [kernel_plan(): pl.pallas_call(block_kernel, out_shape=(shape((CORES, levels, PARTS, deep...]
where the time goes in v3:
time: 188 us; the launch traced here: 186 us
  Pallas kernels  184 us (98%)
    pallas_call x1, Pallas kernels, kernel_plan(): pl.pallas_call(block_kernel, out_shape=(shape((CORES, levels, PARTS, deep...  172 us
    pallas_call x1, Pallas kernels, kernel_plan(): pl.pallas_call(functools.partial(update_kernel, 2.0 * width * hidden_unit...  12.6 us

profile of v3, /device:TPU:0, one launch (start us, length us, event | category | flops | bytes accessed | tf_op | source)
XLA Modules:
  0.0 186.3 jit_solution(9305524977108227614)
XLA Ops:
  0.6 1.3 reshape.19.gain
  1.9 171.6 %shard_map.147 = (bf16[2,4,2,80,1280]{4,3,2,1,0:T(8,128)(2,1)}, f32[8,128]{1,0:T(8,128)}) custom-call(f32[320,2560]{1,0:T(8,128)} %up.1, f32[320,2560]{1,0:T(8,128)} %down.1, bf16[512,1280]{1,0:T(8,128)(2,1)} %tokens.1, bf16[512,1280]{1,0:T(8,128)(2,1)} %out_grad.1, s32[1,512]{1,0:T(1,128)} %seg.1, s32[1,512]{1,0:T(1,128)} %bitcast.2, s32[1,512]{1,0:T(1,128)} %bitcast.3, ...), custom_call_target="tpu_custom_call" | custom-call | flops 13421772800 | bytes 10485760 | tf_op jit(solution)/shard_map/pallas_call | solution.py:329
  173.5 12.6 %shard_map.148 = (f32[320,2560]{1,0:T(8,128)}, f32[320,2560]{1,0:T(8,128)}, f32[320,2560]{1,0:T(8,128)}, f32[320,2560]{1,0:T(8,128)}) custom-call(bf16[2,4,2,80,1280]{4,3,2,1,0:T(8,128)(2,1)} %get-tuple-element.6.grads, f32[8,128]{1,0:T(8,128)} %get-tuple-element.7.squares, f32[320,2560]{1,0:T(8,128)} %up.1, f32[320,2560]{1,0:T(8,128)} %down.1, ...), custom_call_target="tpu_custom_call" | custom-call | flops 6553600 | bytes 27852800 | tf_op jit(solution)/shard_map/pallas_call | solution.py:375

commit v4 on v3

--- a/solution.py
+++ b/solution.py
@@ -86,34 +86,34 @@
     above = [(gx, ahead[k] * PAIR + l) for k in range(levels)]
     greet([partner, across, diagonal, beside] + above[1:])
     copies = Copies(send, recv)
-    half = shard.shape[3]
-    widths = chunk_widths(half)
+    half = master_up.shape[1] // CORES
+    widths = [piece.shape[3] for piece in shard]
     chunks = len(widths)
-    at = [pl.ds(sum(widths[:q]), widths[q]) for q in range(chunks)]
+    offset = [sum(widths[:q]) for q in range(chunks)]
     count, features = tokens.shape
-    block = s1.shape[2]
+    block = s1[0].shape[2]
     deep = block // levels
 
     straight, crossed, near, passed = {}, {}, {}, {}
 
     def send_weights(q):
         for k in range(CORES):
-            start = k * half + at[q].start
-            shard[k, 0, :, at[q]] = master_up[:, start : start + widths[q]].astype(bf16)
-            shard[k, 1, :, at[q]] = master_down[:, start : start + widths[q]].astype(bf16)
-        mine = full.at[odd, gx, :, at[q]]
-        straight[q] = copies.start(shard.at[c, odd, :, at[q]], mine, across)
-        crossed[q] = copies.start(shard.at[1 - c, odd, :, at[q]], mine, diagonal)
+            start = k * half + offset[q]
+            shard[q][k, 0, :, :] = master_up[:, start : start + widths[q]].astype(bf16)
+            shard[q][k, 1, :, :] = master_down[:, start : start + widths[q]].astype(bf16)
+        mine = full[q].at[odd, gx]
+        straight[q] = copies.start(shard[q].at[c, odd], mine, across)
+        crossed[q] = copies.start(shard[q].at[1 - c, odd], mine, diagonal)
         near[q] = copies.start(
-            shard.at[1 - c, :, :, at[q]], full.at[:, gx, :, at[q]], partner
+            shard[q].at[1 - c], full[q].at[:, gx], partner
         )
         for u in range(PARTS):
-            full[u, gx, :, at[q]] = shard[c, u, :, at[q]]
+            full[q][u, gx, :, :] = shard[q][c, u, :, :]
 
     def pass_weights(q):
         for k, (arrived, owner) in enumerate(((straight[q], across[0]), (crossed[q], diagonal[0]))):
             arrived.wait_recv()
-            piece = full.at[odd, owner, :, at[q]]
+            piece = full[q].at[odd, owner]
             passed[q, k] = copies.start(piece, piece, neighbour)
 
     def column(row, lanes):
@@ -158,17 +158,17 @@
         def _(i):
             own = pl.ds(pl.multiple_of(i * tile, tile), tile)
             v = jnp.dot(
-                normed[own, :], full[0, :, :, at[q]].reshape(features, width), preferred_element_type=f32
+                normed[own, :], full[q][0, :, :, :].reshape(features, width), preferred_element_type=f32
             )
             grad = jnp.dot(
-                weighted[own, :], full[1, :, :, at[q]].reshape(features, width), preferred_element_type=f32
+                weighted[own, :], full[q][1, :, :, :].reshape(features, width), preferred_element_type=f32
             )
             square = v * v
             t = jnp.tanh(0.7978845608 * (v + 0.044715 * (square * v)))
             rising = 0.5 * (1.0 + t)
             slope = 0.7978845608 * (1.0 + 3.0 * 0.044715 * square)
-            hidden[own, at[q]] = (v * rising).astype(bf16)
-            pre_grad[own, at[q]] = (grad * (rising + 0.5 * v * (1.0 - t * t) * slope)).astype(bf16)
+            hidden[q][own, :] = (v * rising).astype(bf16)
+            pre_grad[q][own, :] = (grad * (rising + 0.5 * v * (1.0 - t * t) * slope)).astype(bf16)
 
     def product(p, q, at_x, at_l):
         own = pl.ds(pl.multiple_of((at_x * PAIR + at_l) * block, 16), block)
@@ -176,7 +176,7 @@
         return sum(
             jnp.dot(
                 left[k, own, :],
-                right[k * count : (k + 1) * count, at[q]],
+                right[q][k * count : (k + 1) * count, :],
                 preferred_element_type=f32,
             )
             for k in range(CORES)
@@ -189,45 +189,45 @@
         for slot in range(2):
             for p in range(PARTS):
                 where = (1 - x, 1 - l) if slot == 0 else ((1 - x, l), (x, 1 - l))[p]
-                s1[p, slot, :, at[q]] = product(p, q, *where).astype(bf16)
+                s1[q][p, slot, :, :] = product(p, q, *where).astype(bf16)
                 first[q, p, slot] = copies.start(
-                    s1.at[p, slot, :, at[q]], r1.at[p, slot, :, at[q]], targets[p]
+                    s1[q].at[p, slot], r1[q].at[p, slot], targets[p]
                 )
 
     def send_second(q):
         for p in range(PARTS):
             own = product(p, q, *((x, 1 - l), (1 - x, l))[p])
             first[q, p, 0].wait_recv()
-            s2[p, :, at[q]] = (own + r1[p, 0, :, at[q]].astype(f32)).astype(bf16)
-            second[q, p] = copies.start(s2.at[p, :, at[q]], r2.at[p, :, at[q]], targets[1 - p])
+            s2[q][p, :, :] = (own + r1[q][p, 0, :, :].astype(f32)).astype(bf16)
+            second[q, p] = copies.start(s2[q].at[p], r2[q].at[p], targets[1 - p])
 
     def send_third(q):
         for p in range(PARTS):
             own = product(p, q, x, l)
             first[q, p, 1].wait_recv()
             second[q, p].wait_recv()
-            total = own + r1[p, 1, :, at[q]].astype(f32) + r2[p, :, at[q]].astype(f32)
+            total = own + r1[q][p, 1, :, :].astype(f32) + r2[q][p, :, :].astype(f32)
             for level in range(levels):
                 piece = total[level * deep : (level + 1) * deep]
-                keep[level, p, :, at[q]] = piece
-                s3[level, p, :, at[q]] = piece.astype(bf16)
+                keep[q][level, p, :, :] = piece
+                s3[q][level, p, :, :] = piece.astype(bf16)
         for k in range(1, levels):
             third[q, k] = copies.start(
-                s3.at[ahead[k], :, :, at[q]], r3.at[h, :, :, at[q]], above[k]
+                s3[q].at[ahead[k]], r3[q].at[h], above[k]
             )
 
     def send_whole(q):
         for k in range(1, levels):
             third[q, k].wait_recv()
         for p in range(PARTS):
-            total = keep[h, p, :, at[q]]
+            total = keep[q][h, p, :, :]
             for k in range(1, levels):
-                total = total + r3[behind[k], p, :, at[q]].astype(f32)
-            whole[l, h, p, :, at[q]] = total.astype(bf16)
+                total = total + r3[q][behind[k], p, :, :].astype(f32)
+            whole[q][l, h, p, :, :] = total.astype(bf16)
             power = jnp.sum((total * total).reshape(deep // 8, 8, widths[q]), axis=0)
             for lane in range(widths[q] // 128):
                 ss[...] += power[:, lane * 128 : (lane + 1) * 128]
-        piece = whole.at[l, h, :, :, at[q]]
+        piece = whole[q].at[l, h]
         for k in range(1, levels):
             spread[q, k] = copies.start(piece, piece, above[k])
         beyond[q, 0] = copies.start(piece, piece, beside)
@@ -235,21 +235,22 @@
     def pass_whole(q):
         for k in range(1, levels):
             spread[q, k].wait_recv()
-            piece = whole.at[l, behind[k], :, :, at[q]]
+            piece = whole[q].at[l, behind[k]]
             beyond[q, k] = copies.start(piece, piece, beside)
 
     def send_last(q):
         for k in range(levels):
             beyond[q, k].wait_recv()
         last[q] = copies.start(
-            whole.at[1 - c, :, :, :, at[q]], out.at[c, :, :, :, at[q]], partner
+            whole[q].at[1 - c], out[q].at[c], partner
         )
-        out[c, :, :, :, at[q]] = whole[c, :, :, :, at[q]]
+        out[q][c, :, :, :, :] = whole[q][c, :, :, :, :]
 
     def add_squares():
         ss_s[0] = ss[...]
         waits = [copies.start(ss_s.at[0], ss_r.at[h], above[k]) for k in range(1, levels)]
         ss_r[h] = ss[...]
+        yield
         for copy in waits:
             copy.wait_recv()
         running = ss_r[0]
@@ -257,12 +258,15 @@
             running = running + ss_r[level]
         for turn, target in enumerate((beside, across, partner)):
             ss_s[1 + turn] = running
-            copies.start(ss_s.at[1 + turn], ss_r.at[levels + turn], target).wait_recv()
+            copy = copies.start(ss_s.at[1 + turn], ss_r.at[levels + turn], target)
+            yield
+            copy.wait_recv()
             running = running + ss_r[levels + turn]
         squares[...] = running
 
     ss[...] = jnp.zeros_like(ss)
     send_weights(0)
+    send_weights(1)
     layer_norm()
     mine = pl.ds(pl.multiple_of(c * count, 128), count)
     shared = [
@@ -270,23 +274,23 @@
         for piece in (normed.at[mine], weighted.at[mine], norm_t.at[c], weight_t.at[c])
     ]
     pass_weights(0)
-    send_weights(1)
     for copy in shared:
         copy.wait_recv()
-    order = (
-        (0, forward), (5, send_last), (4, pass_whole), (3, send_whole),
-        (2, send_third), (1, send_second), (0, send_first),
-    )
+    stages = forward, send_first, send_second, send_third, send_whole, pass_whole, send_last
+    turns = add_squares()
     for tick in range(chunks + 5):
-        if 0 < tick and tick + 1 < chunks:
-            send_weights(tick + 1)
-        for lag, action in order:
+        if tick + 2 < chunks:
+            send_weights(tick + 2)
+        if tick + 1 < chunks:
+            pass_weights(tick + 1)
+        for stage, action in enumerate(stages):
+            lag = max(stage - 1, 0)
             if 0 <= tick - lag < chunks:
                 action(tick - lag)
-            if lag == 0 and action is forward and tick + 1 < chunks:
-                pass_weights(tick + 1)
-        if tick == chunks + 2:
-            add_squares()
+        if tick >= chunks + 2:
+            next(turns)
+    for _ in turns:
+        pass
     for q in range(chunks):
         last[q].wait_recv()
     copies.finish()
@@ -296,13 +300,16 @@
     entries, grads, squares, up, down, moment_up, moment_down, new_up, new_down, new_mu, new_md
 ):
     scale = lax.rsqrt(jnp.sum(squares[...]) / entries + 1e-06)
-    for p, old, moment, new, new_moment in (
-        (0, up, moment_up, new_up, new_mu),
-        (1, down, moment_down, new_down, new_md),
-    ):
-        fresh = momentum_keep * moment[...] + scale * grads[0, 0, p].astype(jnp.float32)
-        new_moment[...] = fresh
-        new[...] = old[...] - learn_rate * fresh
+    end = 0
+    for grad in grads:
+        start, end = end, end + grad.shape[4]
+        for p, old, moment, new, new_moment in (
+            (0, up, moment_up, new_up, new_mu),
+            (1, down, moment_down, new_down, new_md),
+        ):
+            fresh = momentum_keep * moment[:, start:end] + scale * grad[0, 0, p].astype(jnp.float32)
+            new_moment[:, start:end] = fresh
+            new[:, start:end] = old[:, start:end] - learn_rate * fresh
 
 
 def cost(flops, moved):
@@ -323,31 +330,39 @@
     both = CORES * count
     block = width // (gx // CORES) // PAIR
     deep = block // levels
-    chunks = len(chunk_widths(half))
+    widths = chunk_widths(half)
+    chunks = len(widths)
+
+    def split(*lead):
+        return [VMEM(lead + (w,), bf16) for w in widths]
+
     vm = pl.BlockSpec(memory_space=VMEM)
     n_copies = chunks * (11 + 2 * (levels - 1) + levels + 1) + 4 + levels + 2
     grads, squares = pl.pallas_call(
         block_kernel,
-        out_shape=(shape((CORES, levels, PARTS, deep, half), bf16), shape((8, 128), f32)),
+        out_shape=(
+            [shape((CORES, levels, PARTS, deep, w), bf16) for w in widths],
+            shape((8, 128), f32),
+        ),
         in_specs=[vm] * 10,
-        out_specs=(vm, vm),
+        out_specs=([vm] * chunks, vm),
         scratch_shapes=[
-            VMEM((CORES, PARTS, depth, half), bf16),
-            VMEM((PARTS, gx, depth, half), bf16),
+            split(CORES, PARTS, depth),
+            split(PARTS, gx, depth),
             VMEM((both, width), bf16),
             VMEM((both, width), bf16),
             VMEM((CORES, width, count), bf16),
             VMEM((CORES, width, count), bf16),
-            VMEM((both, half), bf16),
-            VMEM((both, half), bf16),
-            VMEM((PARTS, 2, block, half), bf16),
-            VMEM((PARTS, 2, block, half), bf16),
-            VMEM((PARTS, block, half), bf16),
-            VMEM((PARTS, block, half), bf16),
-            VMEM((levels, PARTS, deep, half), bf16),
-            VMEM((levels, PARTS, deep, half), bf16),
-            VMEM((levels, PARTS, deep, half), f32),
-            VMEM((PAIR, levels, PARTS, deep, half), bf16),
+            split(both),
+            split(both),
+            split(PARTS, 2, block),
+            split(PARTS, 2, block),
+            split(PARTS, block),
+            split(PARTS, block),
+            split(levels, PARTS, deep),
+            split(levels, PARTS, deep),
+            [VMEM((levels, PARTS, deep, w), f32) for w in widths],
+            split(PAIR, levels, PARTS, deep),
             VMEM((8, 128), f32),
             VMEM((4, 8, 128), f32),
             VMEM((levels + 3, 8, 128), f32),
@@ -377,7 +392,10 @@
         grid=(levels, CORES),
         out_shape=(shape(master_up.shape, f32),) * 4,
         in_specs=[
-            pl.BlockSpec((1, 1, PARTS, deep, half), lambda i, j: (j, i, 0, 0, 0)),
+            [
+                pl.BlockSpec((1, 1, PARTS, deep, w), lambda i, j: (j, i, 0, 0, 0))
+                for w in widths
+            ],
             pl.BlockSpec((8, 128), lambda i, j: (0, 0)),
             flat, flat, flat, flat,
         ],

time: 188 us -> 166 us (0.88)
  Pallas kernels: 184 us -> 164 us
    pallas_call x1, Pallas kernels: 172 us -> 151 us  [kernel_plan(): pl.pallas_call(block_kernel, out_shape=([shape((CORES, levels, PARTS, dee...]
where the time goes in v4:
time: 166 us
  Pallas kernels  164 us (99%)
    pallas_call x1, Pallas kernels, kernel_plan(): pl.pallas_call(block_kernel, out_shape=([shape((CORES, levels, PARTS, dee...  151 us
    pallas_call x1, Pallas kernels, kernel_plan(): pl.pallas_call(functools.partial(update_kernel, 2.0 * width * hidden_unit...  12.6 us

profile of v4, /device:TPU:0, one launch (start us, length us, event | category | flops | bytes accessed | tf_op | source)
XLA Modules:
  0.0 165.9 jit_solution(11052414040956982516)
XLA Ops:
  0.6 1.3 reshape.19.gain
  1.9 151.2 %shard_map.147 = (bf16[2,4,2,80,128]{4,3,2,1,0:T(8,128)(2,1)}, bf16[2,4,2,80,256]{4,3,2,1,0:T(8,128)(2,1)}, bf16[2,4,2,80,256]{4,3,2,1,0:T(8,128)(2,1)}, bf16[2,...) custom-call(f32[320,2560]{1,0:T(8,128)} %up.1, ...), custom_call_target="tpu_custom_call" | custom-call | flops 13421772800 | bytes 10485760 | tf_op jit(solution)/shard_map/pallas_call | solution.py:341
  153.1 12.6 %shard_map.148 = (f32[320,2560]{1,0:T(8,128)}, f32[320,2560]{1,0:T(8,128)}, f32[320,2560]{1,0:T(8,128)}, f32[320,2560]{1,0:T(8,128)}) custom-call(bf16[2,4,2,80,128]{4,3,2,1,0:T(8,128)(2,1)} %get-tuple-element.11.grads_0_, bf16[2,4,2,80,256]{4,3,2,1,0:T(8,128)(2,1)} %get-tuple-element.12.grads_1_, bf16[2,4,2,80,256]{4,3,2,1,0:T(8,128)(2,1)} %get-tuple-element.13.grads_2_, ...), custom_call_target="tpu_custom_call" | custom-call | flops 6553600 | bytes 27852800 | tf_op jit(solution)/shard_map/pallas_call | solution.py:390

commit v5 on v4

--- a/solution.py
+++ b/solution.py
@@ -26,9 +26,9 @@
 
 
 def chunk_widths(columns):
-    if columns % 256 or columns < 512:
+    if columns % 256 or columns < 768:
         return [128] * (columns // 128)
-    return [128] + [256] * (columns // 256 - 1) + [128]
+    return [128] * 2 + [256] * (columns // 256 - 2) + [128] * 2
 
 
 class Copies:
@@ -138,13 +138,15 @@
             average = jnp.mean(embedded, axis=1, keepdims=True)
             centered = embedded - average
             variance = jnp.mean(centered * centered, axis=1, keepdims=True)
-            left = (centered * lax.rsqrt(variance + 1e-06) * gain[...]).astype(bf16)
+            left = (centered * lax.rsqrt(variance + 1e-06) * gain[...].reshape(1, features)).astype(bf16)
             normed[own, :] = left
             norm_t[c, :, span] = left.T
             weight = column(token_weight[:, span], 128)[:, :1]
             right = (out_grad[span, :].astype(f32) * weight).astype(bf16)
             weighted[own, :] = right
             weight_t[c, :, span] = right.T
+            for piece in (normed.at[own], weighted.at[own]):
+                shared.append(copies.start(piece, piece, partner))
 
     def forward(q):
         near[q].wait_recv()
@@ -267,12 +269,9 @@
     ss[...] = jnp.zeros_like(ss)
     send_weights(0)
     send_weights(1)
+    shared = []
     layer_norm()
-    mine = pl.ds(pl.multiple_of(c * count, 128), count)
-    shared = [
-        copies.start(piece, piece, partner)
-        for piece in (normed.at[mine], weighted.at[mine], norm_t.at[c], weight_t.at[c])
-    ]
+    turned = [copies.start(piece, piece, partner) for piece in (norm_t.at[c], weight_t.at[c])]
     pass_weights(0)
     for copy in shared:
         copy.wait_recv()
@@ -287,6 +286,9 @@
             lag = max(stage - 1, 0)
             if 0 <= tick - lag < chunks:
                 action(tick - lag)
+            if tick == 0 and action is forward:
+                for copy in turned:
+                    copy.wait_recv()
         if tick >= chunks + 2:
             next(turns)
     for _ in turns:
@@ -337,7 +339,7 @@
         return [VMEM(lead + (w,), bf16) for w in widths]
 
     vm = pl.BlockSpec(memory_space=VMEM)
-    n_copies = chunks * (11 + 2 * (levels - 1) + levels + 1) + 4 + levels + 2
+    n_copies = chunks * (11 + 2 * (levels - 1) + levels + 1) + count // 64 + levels + 4
     grads, squares = pl.pallas_call(
         block_kernel,
         out_shape=(
@@ -383,7 +385,7 @@
         pos_cols.reshape(1, count),
         row_table,
         col_table,
-        norm_gain.reshape(1, width),
+        norm_gain,
     )
 
     flat = pl.BlockSpec((deep, half), lambda i, j: (i, j))

time: 166 us -> 164 us (0.988)
  Pallas kernels: 164 us -> 161 us
    pallas_call x1, Pallas kernels: 151 us -> 149 us  [kernel_plan(): pl.pallas_call(block_kernel, out_shape=([shape((CORES, levels, PARTS, dee...]
where the time goes in v5:
time: 164 us; the launch traced here: 162 us
  Pallas kernels  161 us (98%)
    pallas_call x1, Pallas kernels, kernel_plan(): pl.pallas_call(block_kernel, out_shape=([shape((CORES, levels, PARTS, dee...  149 us
    pallas_call x1, Pallas kernels, kernel_plan(): pl.pallas_call(functools.partial(update_kernel, 2.0 * width * hidden_unit...  12.6 us

profile of v5, /device:TPU:0, one launch (start us, length us, event | category | flops | bytes accessed | tf_op | source)
XLA Modules:
  0.0 162.3 jit_solution(7499728680446560354)
XLA Ops:
  0.6 148.9 %shard_map.147 = (bf16[2,4,2,80,128]{4,3,2,1,0:T(8,128)(2,1)}, bf16[2,4,2,80,128]{4,3,2,1,0:T(8,128)(2,1)}, bf16[2,4,2,80,256]{4,3,2,1,0:T(8,128)(2,1)}, bf16[2,...) custom-call(f32[320,2560]{1,0:T(8,128)} %up.1, ...), custom_call_target="tpu_custom_call" | custom-call | flops 13421772800 | bytes 10485760 | tf_op jit(solution)/shard_map/pallas_call | solution.py:343
  149.6 12.6 %shard_map.148 = (f32[320,2560]{1,0:T(8,128)}, f32[320,2560]{1,0:T(8,128)}, f32[320,2560]{1,0:T(8,128)}, f32[320,2560]{1,0:T(8,128)}) custom-call(bf16[2,4,2,80,128]{4,3,2,1,0:T(8,128)(2,1)} %get-tuple-element.12.grads_0_, bf16[2,4,2,80,128]{4,3,2,1,0:T(8,128)(2,1)} %get-tuple-element.13.grads_1_, bf16[2,4,2,80,256]{4,3,2,1,0:T(8,128)(2,1)} %get-tuple-element.14.grads_2_, ...), custom_call_target="tpu_custom_call" | custom-call | flops 6553600 | bytes 27852800 | tf_op jit(solution)/shard_map/pallas_call | solution.py:392

commit v6 on v5

--- a/solution.py
+++ b/solution.py
@@ -67,10 +67,10 @@
 
 
 def block_kernel(
-    master_up, master_down, tokens, out_grad, seg, rows, cols, row_table, col_table, gain,
+    up_home, down_home, tokens, out_grad, seg, rows, cols, row_table, col_table, gain,
     out, squares,
     shard, full, normed, weighted, norm_t, weight_t, pre_grad, hidden,
-    s1, r1, s2, r2, s3, r3, keep, whole, ss, ss_s, ss_r, send, recv,
+    s1, r1, s2, r2, s3, r3, keep, whole, ss, ss_s, ss_r, master_up, master_down, fetch, send, recv,
 ):
     bf16, f32 = jnp.bfloat16, jnp.float32
     gx, gy, x, c, h, l = place()
@@ -84,11 +84,22 @@
     ahead = [lax.rem(h + k, levels) for k in range(levels)]
     behind = [lax.rem(h + levels - k, levels) for k in range(levels)]
     above = [(gx, ahead[k] * PAIR + l) for k in range(levels)]
-    greet([partner, across, diagonal, beside] + above[1:])
-    copies = Copies(send, recv)
     half = master_up.shape[1] // CORES
     widths = [piece.shape[3] for piece in shard]
     chunks = len(widths)
+    early = widths[0] + widths[1]
+    fetched = []
+    for lo, hi in ((0, early), (early, half)):
+        for k in range(CORES):
+            for home, here in ((up_home, master_up), (down_home, master_down)):
+                span = pl.ds(k * half + lo, hi - lo)
+                copy = pltpu.make_async_copy(
+                    home.at[:, span], here.at[:, span], fetch.at[len(fetched)]
+                )
+                copy.start()
+                fetched.append(copy)
+    greet([partner, across, diagonal, beside] + above[1:])
+    copies = Copies(send, recv)
     offset = [sum(widths[:q]) for q in range(chunks)]
     count, features = tokens.shape
     block = s1[0].shape[2]
@@ -267,8 +278,12 @@
         squares[...] = running
 
     ss[...] = jnp.zeros_like(ss)
+    for copy in fetched[: 2 * CORES]:
+        copy.wait()
     send_weights(0)
     send_weights(1)
+    for copy in fetched[2 * CORES :]:
+        copy.wait()
     shared = []
     layer_norm()
     turned = [copies.start(piece, piece, partner) for piece in (norm_t.at[c], weight_t.at[c])]
@@ -346,7 +361,7 @@
             [shape((CORES, levels, PARTS, deep, w), bf16) for w in widths],
             shape((8, 128), f32),
         ),
-        in_specs=[vm] * 10,
+        in_specs=[pl.BlockSpec(memory_space=pl.ANY)] * 2 + [vm] * 8,
         out_specs=([vm] * chunks, vm),
         scratch_shapes=[
             split(CORES, PARTS, depth),
@@ -368,6 +383,9 @@
             VMEM((8, 128), f32),
             VMEM((4, 8, 128), f32),
             VMEM((levels + 3, 8, 128), f32),
+            VMEM(master_up.shape, f32),
+            VMEM(master_down.shape, f32),
+            pltpu.SemaphoreType.DMA((4 * CORES,)),
             pltpu.SemaphoreType.DMA((n_copies,)),
             pltpu.SemaphoreType.DMA((n_copies,)),
         ],

time: 164 us -> 161 us (0.982)
    pallas_call x1, Pallas kernels: 149 us -> 147 us  [kernel_plan(): pl.pallas_call(block_kernel, out_shape=([shape((CORES, levels, PARTS, dee...]
where the time goes in v6:
time: 161 us; the launch traced here: 160 us
  Pallas kernels  160 us (99%)
    pallas_call x1, Pallas kernels, kernel_plan(): pl.pallas_call(block_kernel, out_shape=([shape((CORES, levels, PARTS, dee...  147 us
    pallas_call x1, Pallas kernels, kernel_plan(): pl.pallas_call(functools.partial(update_kernel, 2.0 * width * hidden_unit...  12.6 us

profile of v6, /device:TPU:0, one launch (start us, length us, event | category | flops | bytes accessed | tf_op | source)
XLA Modules:
  0.0 160.4 jit_solution(9096480368412037621)
XLA Ops:
  0.6 147.0 %shard_map.147 = (bf16[2,4,2,80,128]{4,3,2,1,0:T(8,128)(2,1)}, bf16[2,4,2,80,128]{4,3,2,1,0:T(8,128)(2,1)}, bf16[2,4,2,80,256]{4,3,2,1,0:T(8,128)(2,1)}, bf16[2,...) custom-call(f32[320,2560]{1,0:T(8,128)} %up.1, ...), custom_call_target="tpu_custom_call" | custom-call | flops 13421772800 | bytes 10485760 | tf_op jit(solution)/shard_map/pallas_call | solution.py:358
  147.6 12.6 %shard_map.148 = (f32[320,2560]{1,0:T(8,128)}, f32[320,2560]{1,0:T(8,128)}, f32[320,2560]{1,0:T(8,128)}, f32[320,2560]{1,0:T(8,128)}) custom-call(bf16[2,4,2,80,128]{4,3,2,1,0:T(8,128)(2,1)} %get-tuple-element.12.grads_0_, bf16[2,4,2,80,128]{4,3,2,1,0:T(8,128)(2,1)} %get-tuple-element.13.grads_1_, bf16[2,4,2,80,256]{4,3,2,1,0:T(8,128)(2,1)} %get-tuple-element.14.grads_2_, ...), custom_call_target="tpu_custom_call" | custom-call | flops 6553600 | bytes 27852800 | tf_op jit(solution)/shard_map/pallas_call | solution.py:410
